TPU v7x, 128 devices: a whole 4x4x4 slice. The times are simulated.
128 devices in a mesh: dp: 2 (over y_hi), seq: 16 (over y_lo, x, core), tensor: 4 (over z).
Axes of the slice: x: 4, y: 4 (y_hi: 2, y_lo: 2; y = y_hi * 2 + y_lo), z: 4, core: 2. Of those that a mesh axis runs over, the one named last changes fastest.
Arguments:
- queries: bfloat16 [2, 12, 64, 32768], P('dp', 'tensor', None, 'seq'), may hold values from -6 to 6
- key_states: bfloat16 [2, 12, 64, 32768], P('dp', 'tensor', None, 'seq'), may hold values from -6 to 6
- value_states: bfloat16 [2, 12, 64, 32768], P('dp', 'tensor', None, 'seq'), may hold values from -6 to 6
- out_weight: bfloat16 [768, 768], P('tensor'), may hold values from -0.21875 to 0.21875
- grad_output: bfloat16 [2, 32768, 768], P('dp', 'seq'), may hold values from -6 to 6
- phases: int32 [12], P('tensor'), may hold values from 0 to 15
- valid_rows: int32 [2], P('dp'), may hold values from 8192 to 32768
Outputs:
- grad_queries: bfloat16 [2, 12, 64, 32768], P('dp', 'tensor', None, 'seq')
- grad_keys: bfloat16 [2, 12, 64, 32768], P('dp', 'tensor', None, 'seq')
- grad_values: bfloat16 [2, 12, 64, 32768], P('dp', 'tensor', None, 'seq')
- grad_weight: float32 [768, 768], P('tensor')
All inputs are finite; a program needn't handle non-finite values.
Results may differ from a plain program's by a relative error of at most 0.017.
Values may be sent and summed in bfloat16 or wider, within the bound.
A program may use at most 128 MiB of HBM per device.

v0:
```python
import jax
import jax.numpy as jnp
from jax import lax
from jax.sharding import PartitionSpec as P

SEG = 1024
RATE = 16
BLK = 32


NEGATIVE = -1e30


def select_rows(matrix, head_phase):
    row_count, col_count = matrix.shape
    blocks = matrix.reshape(row_count // (RATE * BLK), RATE, BLK, col_count)
    picked = lax.dynamic_index_in_dim(blocks, head_phase, 1, keepdims=False)
    return picked.reshape(row_count // RATE, col_count)


def place_rows(full_rows, picked, head_phase):
    row_count, col_count = full_rows.shape
    blocks = full_rows.reshape(row_count // (RATE * BLK), RATE, BLK, col_count)
    inserted = picked.reshape(row_count // (RATE * BLK), 1, BLK, col_count)
    return lax.dynamic_update_slice_in_dim(blocks, inserted, head_phase, 1).reshape(
        row_count, col_count
    )


def product(form, left, right):
    return jnp.einsum(form, left, right, preferred_element_type=jnp.float32)


def level_forward(query_in, key_in, value_in, allowed):
    score_scale = query_in.shape[-1] ** (-0.5)
    scores = product("...id,...jd->...ij", query_in, key_in) * score_scale
    scores = jnp.where(allowed, scores, NEGATIVE)
    row_max = jnp.max(scores, axis=-1, keepdims=True)
    lse = row_max + jnp.log(jnp.sum(jnp.exp(scores - row_max), axis=-1, keepdims=True))
    probs = jnp.exp(scores - lse).astype(jnp.bfloat16)
    output = product("...ij,...jd->...id", probs, value_in)
    return (output, lse[..., 0], probs)


def level_backward(query_in, key_in, value_in, probs, output, dout, dlse):
    score_scale = query_in.shape[-1] ** (-0.5)
    delta = jnp.sum(dout.astype(jnp.float32) * output, axis=-1)
    prob_grad = product("...id,...jd->...ij", dout, value_in)
    score_grad = (probs.astype(jnp.float32) * (prob_grad + (dlse - delta)[..., None])).astype(
        jnp.bfloat16
    )
    query_grad = product("...ij,...jd->...id", score_grad, key_in) * score_scale
    key_grad = product("...ij,...id->...jd", score_grad, query_in) * score_scale
    value_grad = product("...ij,...id->...jd", probs, dout)
    return (query_grad, key_grad, value_grad)


def shards(queries, key_states, value_states, out_weight, grad_output, phases, valid_rows):
    heads_here = phases.shape[0]
    head_size = queries.shape[2]
    row_count = queries.shape[3]
    valid_count = valid_rows[0]
    grad_attn = jnp.einsum(
        "td,cd->tc", grad_output[0], out_weight, preferred_element_type=jnp.float32
    ).astype(jnp.bfloat16)
    query_heads = queries[0].transpose(0, 2, 1)
    key_heads = key_states[0].transpose(0, 2, 1)
    value_heads = value_states[0].transpose(0, 2, 1)
    grad_heads = grad_attn.reshape(row_count, heads_here, head_size).transpose(1, 0, 2)
    key_pick = jax.vmap(select_rows)(key_heads, phases)
    value_pick = jax.vmap(select_rows)(value_heads, phases)
    key_far, value_far = (
        lax.all_gather(key_pick, "seq", axis=1, tiled=True),
        lax.all_gather(value_pick, "seq", axis=1, tiled=True),
    )
    segments = row_count // SEG

    def head_work(query_in, key_in, value_in, cotangent, head_phase, key_remote, value_remote):

        def cut(matrix):
            return matrix.reshape(segments, SEG, head_size)

        far_index = jnp.arange(key_remote.shape[0], dtype=jnp.int32)
        global_rows = far_index // BLK * (RATE * BLK) + head_phase * BLK + far_index % BLK
        allowed_far = (global_rows < valid_count)[None, :]
        near_out, near_lse, near_probs = level_forward(
            cut(query_in), cut(key_in), cut(value_in), True
        )
        near_out = near_out.reshape(row_count, head_size)
        near_lse = near_lse.reshape(row_count, 1)
        query_pick = select_rows(query_in, head_phase)
        far_out, far_lse, far_probs = level_forward(
            query_pick, key_remote, value_remote, allowed_far
        )
        near_pick = select_rows(near_out, head_phase)
        mixing = jax.nn.sigmoid(far_lse - select_rows(near_lse, head_phase)[:, 0])
        combined = place_rows(
            near_out, near_pick + mixing[:, None] * (far_out - near_pick), head_phase
        )
        grad_full = cotangent.astype(jnp.float32)
        grad_pick = select_rows(grad_full, head_phase)
        mix_grad = jnp.sum(grad_pick * (far_out - near_pick), axis=1)
        far_dlse = mix_grad * mixing * (1.0 - mixing)
        far_dout = (mixing[:, None] * grad_pick).astype(jnp.bfloat16)
        near_dout = place_rows(grad_full, (1.0 - mixing)[:, None] * grad_pick, head_phase).astype(
            jnp.bfloat16
        )
        near_dlse = place_rows(
            jnp.zeros((row_count, 1), jnp.float32), -far_dlse[:, None], head_phase
        )
        near_q, near_k, near_v = level_backward(
            cut(query_in),
            cut(key_in),
            cut(value_in),
            near_probs,
            cut(near_out),
            cut(near_dout),
            near_dlse.reshape(segments, SEG),
        )
        far_q, far_k, far_v = level_backward(
            query_pick, key_remote, value_remote, far_probs, far_out, far_dout, far_dlse
        )
        far_term = far_dlse - jnp.sum(far_dout.astype(jnp.float32) * far_out, axis=-1)
        empty = jnp.zeros((row_count, head_size), jnp.float32)
        query_grad = near_q.reshape(row_count, head_size) + place_rows(empty, far_q, head_phase)
        return (
            combined,
            query_grad,
            near_k.reshape(row_count, head_size),
            near_v.reshape(row_count, head_size),
            far_k,
            far_v,
            query_pick,
            far_dout,
            far_lse,
            far_term,
        )

    (
        combined,
        query_grad,
        key_grad,
        value_grad,
        key_terms,
        value_terms,
        query_pick,
        far_dout,
        far_lse,
        far_term,
    ) = jax.vmap(head_work)(
        query_heads, key_heads, value_heads, grad_heads, phases, key_far, value_far
    )
    empty_heads = jnp.zeros_like(key_grad)
    own_keys, own_values = (
        lax.psum_scatter(key_terms, "seq", scatter_dimension=1, tiled=True),
        lax.psum_scatter(value_terms, "seq", scatter_dimension=1, tiled=True),
    )
    key_grad = key_grad + jax.vmap(place_rows)(empty_heads, own_keys, phases)
    value_grad = value_grad + jax.vmap(place_rows)(empty_heads, own_values, phases)
    attn_out = (
        combined.transpose(1, 0, 2).reshape(row_count, heads_here * head_size).astype(jnp.bfloat16)
    )
    weight_term = jnp.einsum(
        "tc,td->cd", attn_out, grad_output[0], preferred_element_type=jnp.float32
    )
    grad_weight = lax.psum(weight_term, ("dp", "seq"))
    grad_queries = query_grad.astype(jnp.bfloat16).transpose(0, 2, 1)[None]
    grad_keys = key_grad.astype(jnp.bfloat16).transpose(0, 2, 1)[None]
    grad_values = value_grad.astype(jnp.bfloat16).transpose(0, 2, 1)[None]
    return (grad_queries, grad_keys, grad_values, grad_weight)


def solution(mesh):
    in_specs = (
        P("dp", "tensor", None, "seq"),
        P("dp", "tensor", None, "seq"),
        P("dp", "tensor", None, "seq"),
        P("tensor", None),
        P("dp", "seq", None),
        P("tensor"),
        P("dp"),
    )
    out_specs = (
        P("dp", "tensor", None, "seq"),
        P("dp", "tensor", None, "seq"),
        P("dp", "tensor", None, "seq"),
        P("tensor", None),
    )
    return jax.shard_map(shards, mesh=mesh, in_specs=in_specs, out_specs=out_specs, check_vma=False)
```

profile of v0, /device:TPU:1, one launch (start us, length us, event | category | flops | bytes accessed | tf_op | source)
XLA Modules:
  0.0 403.9 jit_solution(7851430429642236566)
XLA Ops:
  15.9 4.2 %copy.105 = f32[3,4,16,32,64]{4,3,1,2,0:T(8,128)} copy(f32[3,4,16,32,64]{4,3,2,1,0:T(8,128)} %bitcast.264) | data formatting | bytes 3145728 | tf_op jit(solution)/shard_map/vmap()/reshape | solution.py:23
  26.6 13.6 %multiply_reduce_fusion = (f32[3,2,1024]{2,1,0:T(2,128)S(1)}, f32[3,2,1024,1024]{2,3,1,0:T(8,128)}) fusion(bf16[3,2,1024,64]{3,2,1,0:T(8,128)(2,1)} %bitcast.272, bf16[3,2,1024,64]{3,2,1,0:T(8,128)(2,1)} %bitcast.275), kind=kOutput, calls=%fused_computation.33 | convolution fusion | flops 817883136 | bytes 26763264 | tf_op jit(solution)/shard_map/vmap(...id,...jd->...ij)/dot_general | solution.py:31
  40.2 10.7 %exponential_reduce_fusion = f32[3,2,1024]{2,1,0:T(2,128)S(1)} fusion(f32[3,2,1024,1024]{2,3,1,0:T(8,128)} %get-tuple-element.210, f32[3,2,1024]{2,1,0:T(2,128)S(1)} %get-tuple-element.209), kind=kLoop, calls=%fused_computation.32 | loop fusion | flops 18868224 | bytes 25214976 | tf_op jit(solution)/shard_map/vmap()/reduce_sum | solution.py:39
  50.9 4.7 %copy-done.1 = f32[3,2,1024,1024]{2,3,1,0:T(8,128)S(1)} copy-done((f32[3,2,1024,1024]{2,3,1,0:T(8,128)S(1)}, f32[3,2,1024,1024]{2,3,1,0:T(8,128)}, u32[]{:S(2)}) %copy-start.1) | copy-done | bytes 25165848
  55.6 7.1 %exponential_convert_fusion = bf16[3,2,1024,1024]{2,3,1,0:T(8,128)(2,1)} fusion(f32[3,2,1024,1024]{2,3,1,0:T(8,128)S(1)} %copy-done.1, f32[3,2,1024]{2,1,0:T(2,128)S(1)} %log_add_fusion), kind=kLoop, calls=%fused_computation.31 | loop fusion | flops 18874368 | bytes 37773312 | tf_op jit(solution)/shard_map/vmap()/convert_element_type | solution.py:40
  73.7 23.4 %all_gather.6 = bf16[3,2048,64]{1,2,0:T(8,128)(2,1)S(1)} all-gather(bf16[3,128,64]{1,2,0:T(8,128)(2,1)S(1)} %copy.102), channel_id=1, replica_groups=mesh['dp'=2,'seq'=16,'tensor'=4] {'seq'}, dimensions={1}, use_global_device_ids=true | all-gather | bytes 835584 | tf_op jit(solution)/shard_map/all_gather | solution.py:73
  100.2 3.5 exponential_convert_fusion.1
  109.8 25.3 %while.6 = (s32[]{:T(128)}, bf16[3,4,16,32,64]{4,3,2,1,0:T(8,128)(2,1)}, s32[3,5]{1,0:T(4,128)S(1)}, bf16[3,4,1,32,64]{4,3,2,1,0:T(8,128)(2,1)S(1)}, s32[]{:T(128)}, /*index=5*/s32[5]{0:T(128)}) while((s32[]{:T(128)}, bf16[3,4,16,32,64]{4,3,2,1,0:T(8,128)(2,1)}, s32[3,5]{1,0:T(4,128)S(1)}, bf16[3,4,1,32,64]{4,3,2,1,0:T(8,128)(2,1)S(1)}, s32[]{:T(128)}, ...), condition=%wide.while_cond, body=%wide.while_body.sunk | while | flops 8213 | bytes 83702 | solution.py:25
  115.0 3.3 fusion.77
  123.4 3.3 fusion.77
  140.0 9.3 %multiply_reduce_fusion.1 = (f32[3,2,1024]{2,1,0:T(2,128)}, f32[3,2,1024,64]{2,3,1,0:T(8,128)}) fusion(bf16[3,2,1024,64]{2,3,1,0:T(8,128)(2,1)} %copy.119, bf16[3,2,1024,1024]{2,3,1,0:T(8,128)(2,1)} %exponential_convert_fusion, bf16[3,2,1024,64]{3,2,1,0:T(8,128)(2,1)} %bitcast.269), kind=kOutput, calls=%fused_computation.49 | convolution fusion | flops 806479872 | bytes 15753216 | tf_op jit(solution)/shard_map/vmap(...ij,...jd->...id)/dot_general | solution.py:31
  149.4 3.3 copy.114
  152.6 4.0 copy.115
  166.6 18.8 %all_gather.7 = bf16[3,2048,64]{1,2,0:T(8,128)(2,1)S(1)} all-gather(bf16[3,128,64]{1,2,0:T(8,128)(2,1)} %copy.111), channel_id=1, replica_groups=mesh['dp'=2,'seq'=16,'tensor'=4] {'seq'}, dimensions={1}, use_global_device_ids=true | all-gather | bytes 835584 | tf_op jit(solution)/shard_map/all_gather | solution.py:74
  194.7 3.5 convert.14
  198.4 23.2 %while.11 = (s32[]{:T(128)}, bf16[3,4,16,32,64]{4,3,2,1,0:T(8,128)(2,1)}, s32[3,5]{1,0:T(4,128)S(1)}, bf16[3,4,1,32,64]{4,3,2,1,0:T(8,128)(2,1)S(1)}, s32[]{:T(128)}, /*index=5*/s32[5]{0:T(128)S(1)}) while((s32[]{:T(128)}, bf16[3,4,16,32,64]{4,3,2,1,0:T(8,128)(2,1)}, s32[3,5]{1,0:T(4,128)S(1)}, bf16[3,4,1,32,64]{4,3,2,1,0:T(8,128)(2,1)S(1)}, ...), condition=%wide.while_cond.5, body=%wide.while_body.5.sunk | while | flops 8213 | bytes 83702 | solution.py:25
  229.3 20.1 %while.7 = (s32[]{:T(128)}, f32[3,4,16,32,1]{3,4,2,1,0:T(1,128)S(1)}, s32[3,5]{1,0:T(4,128)S(1)}, f32[3,4,1,32,1]{3,4,2,1,0:T(1,128)S(1)}, s32[]{:T(128)}, /*index=5*/s32[5]{0:T(128)S(1)}) while((s32[]{:T(128)}, f32[3,4,16,32,1]{3,4,2,1,0:T(1,128)S(1)}, s32[3,5]{1,0:T(4,128)S(1)}, f32[3,4,1,32,1]{3,4,2,1,0:T(1,128)S(1)}, s32[]{:T(128)}, ...), condition=%wide.while_cond.1, body=%wide.while_body.1.sunk | while | flops 149 | bytes 6399 | solution.py:25
  230.0 3.3 concatenate.56
  236.6 3.3 concatenate.56
  243.3 3.3 concatenate.56
  251.0 13.5 %multiply_convert_fusion = bf16[3,2,1024,1024]{2,3,1,0:T(8,128)(2,1)} fusion(bf16[3,2,1024,1024]{2,3,1,0:T(8,128)(2,1)} %exponential_convert_fusion, f32[3,2,1024]{2,1,0:T(2,128)S(1)} %sub.118, bf16[3,2,1024,64]{3,2,1,0:T(8,128)(2,1)} %bitcast.267, bf16[3,2,1024,64]{3,2,1,0:T(8,128)(2,1)} %bitcast.271), kind=kOutput, calls=%fused_computation.30 | convolution fusion | flops 830472192 | bytes 26763264 | tf_op jit(solution)/shard_map/vmap(...id,...jd->...ij)/dot_general | solution.py:31
  264.5 8.6 %multiply_bitcast_fusion.1 = f32[3,2,8,8,1024]{4,3,2,1,0:T(8,128)} fusion(bf16[3,2,1024,1024]{2,3,1,0:T(8,128)(2,1)} %multiply_convert_fusion, bf16[3,2,1024,64]{3,2,1,0:T(8,128)(2,1)} %bitcast.277), kind=kOutput, calls=%fused_computation.48 | convolution fusion | flops 805699584 | bytes 14942208 | tf_op jit(solution)/shard_map/vmap(...ij,...jd->...id)/dot_general | solution.py:31
  273.1 10.1 %multiply_bitcast_fusion = f32[3,2,8,8,1024]{4,3,2,1,0:T(8,128)} fusion(bf16[3,2,1024,1024]{2,3,1,0:T(8,128)(2,1)} %multiply_convert_fusion, bf16[3,2,1024,64]{3,2,1,0:T(8,128)(2,1)} %bitcast.274), kind=kOutput, calls=%fused_computation.46 | convolution fusion | flops 805699584 | bytes 14942208 | tf_op jit(solution)/shard_map/vmap(...ij,...id->...jd)/dot_general | solution.py:31
  283.2 10.2 %convolution_bitcast_fusion = f32[3,2,8,8,1024]{4,3,2,1,0:T(8,128)} fusion(bf16[3,2,1024,1024]{2,3,1,0:T(8,128)(2,1)} %exponential_convert_fusion, bf16[3,2,1024,64]{3,2,1,0:T(8,128)(2,1)} %bitcast.268), kind=kOutput, calls=%fused_computation.50 | convolution fusion | flops 805306368 | bytes 14942208 | tf_op jit(solution)/shard_map/vmap(...ij,...id->...jd)/dot_general | solution.py:31
  298.4 23.3 %while.8 = (s32[]{:T(128)}, f32[3,4,16,32,64]{4,3,2,1,0:T(8,128)}, s32[3,5]{1,0:T(4,128)S(1)}, f32[3,4,1,32,64]{4,3,2,1,0:T(8,128)S(1)}, s32[]{:T(128)}, /*index=5*/s32[5]{0:T(128)S(1)}) while((s32[]{:T(128)}, f32[3,4,16,32,64]{4,3,2,1,0:T(8,128)}, s32[3,5]{1,0:T(4,128)S(1)}, f32[3,4,1,32,64]{4,3,2,1,0:T(8,128)S(1)}, s32[]{:T(128)}, ...), condition=%wide.while_cond.2, body=%wide.while_body.2.sunk | while | flops 8213 | bytes 165622 | solution.py:25
  302.8 3.3 fusion.81
  310.6 3.3 fusion.81
  334.4 22.7 %while.9 = (s32[]{:T(128)}, f32[3,4,16,32,64]{4,3,2,1,0:T(8,128)}, s32[3,5]{1,0:T(4,128)S(1)}, f32[3,4,1,32,64]{4,3,2,1,0:T(8,128)S(1)}, s32[]{:T(128)}, /*index=5*/s32[5]{0:T(128)S(1)}) while((s32[]{:T(128)}, f32[3,4,16,32,64]{4,3,2,1,0:T(8,128)}, s32[3,5]{1,0:T(4,128)S(1)}, f32[3,4,1,32,64]{4,3,2,1,0:T(8,128)S(1)}, s32[]{:T(128)}, ...), condition=%wide.while_cond.3, body=%wide.while_body.3.sunk | while | flops 8213 | bytes 165622 | solution.py:25
  363.4 23.7 %while.10 = (s32[]{:T(128)}, f32[3,4,16,32,64]{4,3,2,1,0:T(8,128)}, s32[3,5]{1,0:T(4,128)S(1)}, f32[3,4,1,32,64]{4,3,2,1,0:T(8,128)S(1)}, s32[]{:T(128)}, /*index=5*/s32[5]{0:T(128)S(1)}) while((s32[]{:T(128)}, f32[3,4,16,32,64]{4,3,2,1,0:T(8,128)}, s32[3,5]{1,0:T(4,128)S(1)}, f32[3,4,1,32,64]{4,3,2,1,0:T(8,128)S(1)}, s32[]{:T(128)}, ...), condition=%wide.while_cond.4, body=%wide.while_body.4.sunk | while | flops 8213 | bytes 165622 | solution.py:25
  368.0 3.4 fusion.85
  375.9 3.4 fusion.85
  383.8 3.4 fusion.85
  (203 shorter events, 205.3 us)
Async XLA Ops:
  8.0 1.9 copy-start
  8.0 323.3 %reduce-scatter.3.cloned.1.call-start = ((), (), s32[]{:S(2)}) async-start(), calls=%async_computation.2 | async-start | bytes 1671168 | tf_op jit(solution)/shard_map/reduce_scatter | solution.py:155
  15.9 4.2 %copy-start.3 = (f32[2048,3,64]{2,0,1:T(8,128)S(1)}, f32[2048,3,64]{2,0,1:T(8,128)}, u32[]{:S(2)}) copy-start(f32[2048,3,64]{2,0,1:T(8,128)} %copy.97) | copy-start | bytes 4718596
  40.2 15.4 %copy-start.1 = (f32[3,2,1024,1024]{2,3,1,0:T(8,128)S(1)}, f32[3,2,1024,1024]{2,3,1,0:T(8,128)}, u32[]{:S(2)}) copy-start(f32[3,2,1024,1024]{2,3,1,0:T(8,128)} %get-tuple-element.210) | copy-start | bytes 75497472
  97.1 1.4 copy-start.6
  98.5 1.7 copy-start.2
  100.1 3.6 copy-start.15
  135.2 4.9 %copy-start.17 = (s32[3,5]{1,0:T(4,128)}, s32[3,5]{1,0:T(4,128)S(1)}, u32[]{:S(2)}) copy-start(s32[3,5]{1,0:T(4,128)S(1)} %get-tuple-element.552) | copy-start | bytes 184
  160.8 24.6 %copy-start.12 = (f32[3,128,64]{1,2,0:T(8,128)S(1)}, f32[3,128,64]{1,2,0:T(8,128)}, u32[]{:S(2)}) copy-start(f32[3,128,64]{1,2,0:T(8,128)} %copy.117) | copy-start | bytes 294916
  166.6 21.6 %copy-start.4 = (bf16[3,128,2048]{2,1,0:T(8,128)(2,1)S(1)}, bf16[3,128,2048]{2,1,0:T(8,128)(2,1)}, u32[]{:S(2)}) copy-start(bf16[3,128,2048]{2,1,0:T(8,128)(2,1)} %exponential_convert_fusion.1) | copy-start | bytes 4718596
  188.8 1.2 copy-start.5
  191.5 168.8 %reduce-scatter.5.cloned.1.call-start = ((), (), s32[]{:S(2)}) async-start(), calls=%async_computation.3 | async-start | bytes 1671168 | tf_op jit(solution)/shard_map/reduce_scatter | solution.py:156
  194.6 200.0 %all-reduce.2.cloned.1.call-start = ((), (), s32[]{:S(2)}) async-start(), calls=%async_computation.4 | async-start | bytes 1179648 | tf_op jit(solution)/shard_map/psum | solution.py:166
  194.6 3.5 copy-start.13
  194.7 3.7 copy-start.18
  194.7 3.7 copy-start.19
  224.0 2.8 copy-start.16
  226.9 24.0 %copy-start.14 = (f32[3,2,1024]{2,1,0:T(2,128)S(1)}, f32[3,2,1024]{2,1,0:T(2,128)}, u32[]{:S(2)}) copy-start(f32[3,2,1024]{2,1,0:T(2,128)} %get-tuple-element.214) | copy-start | bytes 73732
  324.9 2.8 copy-start.11
  327.7 2.0 copy-start.8
  327.7 2.4 copy-start.9
  390.4 3.1 copy-start.7
  390.4 3.1 copy-start.10
Sparse Core Ops, SparseCore 0:
  191.6 58.9 reduce-scatter.2
  253.2 60.8 reduce-scatter.4
Sparse Core Ops, SparseCore 1:
  226.8 102.7 all-reduce.1
where the time goes:
time: 407 us; the launch traced here: 404 us
  local copies, waits for them, and re-layouts  159 us (39%)
  other arithmetic  104 us (26%)
  matrix products  82.1 us (20%)
  blocking collectives  42.2 us (10%)
  between operations  16.4 us (4%)
    dot_general x12, matrix products, product(): return jnp.einsum(form, left, right, preferred_element_type=jnp.float32)  76.3 us
    scatter x54, local copies, waits for them, and re-layouts  69.5 us
    scatter x36, other arithmetic  68.5 us
    all_gather x1, blocking collectives, shards(): lax.all_gather(key_pick, 'seq', axis=1, tiled=True)  23.4 us
    all_gather x1, blocking collectives, shards(): lax.all_gather(value_pick, 'seq', axis=1, tiled=True)  18.8 us
    unnamed x45, local copies, waits for them, and re-layouts  17.7 us
    reshape x4, local copies, waits for them, and re-layouts, select_rows(): blocks = matrix.reshape(row_count // (RATE * BLK), RATE, BLK, col_count)  13.1 us
    gather x6, local copies, waits for them, and re-layouts, select_rows(): picked = lax.dynamic_index_in_dim(blocks, head_phase, 1, keepdims=False)  12.1 us
  transfers between devices with their start and end apart: 3, of which 0 were waited for; matrix products, arithmetic and copies ran while one was open for 50% of the time, Pallas kernels for 0%

commit v1 on v0

v1 whole, which is shorter than its diff:
```python
import jax
import jax.numpy as jnp
from jax import lax
from jax.experimental import pallas as pl
from jax.experimental.pallas import tpu as pltpu
from jax.sharding import PartitionSpec as P

F32 = jnp.float32
BF16 = jnp.bfloat16
SEG = 1024
RATE = 16
BLK = 32
HEADS = 3
DH = 64
ROWS = 2048
SUB = ROWS // RATE
D = 768
PEERS = 16
SPAN = PEERS * SUB
SCALE = 0.125
LOG2E = 1.4426950408889634
QD_ROWS = 144
MESH = pl.DeviceIdType.MESH


def nn(a, b):
    return jnp.dot(a, b, preferred_element_type=F32)


def nt(a, b):
    return lax.dot_general(a, b, (((1,), (1,)), ((), ())), preferred_element_type=F32)


def hi_lo(x):
    hi = x.astype(BF16)
    return hi, (x - hi.astype(F32)).astype(BF16)


def split3(x):
    hi = x.astype(BF16)
    rest = x - hi.astype(F32)
    mid = rest.astype(BF16)
    return hi, mid, (rest - mid.astype(F32)).astype(BF16)


def lanes(n=SUB):
    return lax.broadcasted_iota(jnp.int32, (1, n), 1)


def turn(x, groups):
    groups = groups % 4
    return x if groups == 0 else pltpu.roll(x, groups * 32, 1)


def choose(options, which):
    out = options[0]
    for n in range(1, len(options)):
        out = jnp.where(which == n, options[n], out)
    return out


def pick(load, phase):
    chunk = jnp.full((1, SUB), phase >> 2, jnp.int32)
    part = jnp.full((1, SUB), phase & 3, jnp.int32)
    group = lanes() >> 5
    out = None
    for b in range(4):
        x = choose([load(b * 512 + n * 128).astype(F32) for n in range(4)], chunk)
        x = choose([turn(x, b - n) for n in range(4)], part)
        out = x if b == 0 else jnp.where(group == b, x, out)
    return out


def place_parts(x, phase):
    part = jnp.full((1, SUB), phase & 3, jnp.int32)
    turned = [turn(x, n) for n in range(4)]
    return [choose([turned[(n - b) % 4] for n in range(4)], part) for b in range(4)]


def place_mask(phase, c):
    want = jnp.where((phase >> 2) == (c % 4), phase & 3, -1)
    return (lanes() >> 5) == want


def kernel(
    phases, valid, q_hbm, k_hbm, v_hbm, w_hbm, go_hbm,
    dq_hbm, dk_hbm, dv_hbm, gw_hbm,
    q_s, k_s, v_s, w_s, go_s, g_s, e_s, ds_s, on_s, st_s, nd_s, at_s,
    kv_buf, qd_buf, fe_s, fq_s, fr_s,
    aq_s, ak_s, av_s, oq_s, ok_s, ov_s,
    gw_s, a_send, a_recv, half_s, b_send, b_recv, c_buf, d_buf,
    in_sem, out_sem, kv_send, kv_recv, qd_send, qd_recv, pair_send, pair_recv,
    a_sem, b_ss, b_rs, c_ss, c_rs, d_ss, d_rs,
):
    dp, sq, tz = lax.axis_index("dp"), lax.axis_index("seq"), lax.axis_index("tensor")
    y, x, core = sq // 8, (sq % 8) // 2, sq % 2
    yx = sq // 2
    yg = dp * 2 + y

    copies = [
        pltpu.make_async_copy(k_hbm.at[0], k_s, in_sem.at[0]),
        pltpu.make_async_copy(v_hbm.at[0], v_s, in_sem.at[1]),
        pltpu.make_async_copy(q_hbm.at[0], q_s, in_sem.at[2]),
        pltpu.make_async_copy(w_hbm, w_s, in_sem.at[3]),
        pltpu.make_async_copy(go_hbm.at[0], go_s, in_sem.at[4]),
    ]
    for c in copies:
        c.start()

    def at_yx(k):
        yy, xx = (y + k // 4) % 2, (x + k % 4) % 4
        return yy * 4 + xx

    def from_yx(k):
        yy, xx = (y + 2 - k // 4) % 2, (x + 4 - k % 4) % 4
        return yy * 4 + xx

    same_core = [(dp, at_yx(k) * 2 + core, tz) for k in range(1, 8)]
    sibling = (dp, yx * 2 + 1 - core, tz)
    other_core = [(dp, (y * 4 + (x + k) % 4) * 2 + 1 - core, tz) for k in range(1, 4)]
    y_peers = []
    for k in range(1, 4):
        there = (yg + k) % 4
        y_peers.append((there // 2, (there % 2) * 8 + x * 2 + core, tz))
    barrier = pltpu.get_barrier_semaphore()
    dp_peers = [(1 - dp, yy * 8 + x * 2 + core, tz) for yy in range(2)]
    greet = same_core + [sibling] + other_core + dp_peers
    for peer in greet:
        pl.semaphore_signal(barrier, inc=1, device_id=peer, device_id_type=MESH)

    for c in copies[:2]:
        c.wait()
    for h in range(HEADS):
        ph = phases[h]
        kv_buf[core, yx, h, 0:DH, :] = pick(lambda o: k_s[h, :, pl.ds(o, 128)], ph).astype(BF16)
        kv_buf[core, yx, h, DH:2 * DH, :] = pick(lambda o: v_s[h, :, pl.ds(o, 128)], ph).astype(BF16)
    pl.semaphore_wait(barrier, len(greet))

    def gather(buf, ss, rs):
        sends, recvs = [], []
        for k in range(1, 8):
            mine = buf.at[core, yx]
            sends.append(pltpu.make_async_remote_copy(
                mine, mine, ss.at[k - 1], rs.at[k - 1], device_id=same_core[k - 1], device_id_type=MESH))
            theirs = buf.at[core, from_yx(k)]
            recvs.append(pltpu.make_async_remote_copy(
                theirs, theirs, ss.at[k - 1], rs.at[k - 1], device_id=same_core[k - 1], device_id_type=MESH))
        return sends, recvs

    def to_pair(buf, i):
        out = pltpu.make_async_remote_copy(
            buf.at[core], buf.at[core], pair_send.at[i], pair_recv.at[i], device_id=sibling, device_id_type=MESH)
        back = pltpu.make_async_remote_copy(
            buf.at[1 - core], buf.at[1 - core], pair_send.at[i], pair_recv.at[i], device_id=sibling, device_id_type=MESH)
        return out, back

    kv_out, kv_in = gather(kv_buf, kv_send, kv_recv)
    for c in kv_out:
        c.start()

    copies[2].wait()
    for h in range(HEADS):
        qd_buf[core, yx, h, 0:DH, :] = pick(lambda o: q_s[h, :, pl.ds(o, 128)], phases[h]).astype(BF16)

    def near_forward(u, carry):
        h, off = u // 2, pl.multiple_of((u % 2) * SEG, SEG)
        rows = pl.ds(off, SEG)
        k_t, v_t = k_s[h, :, rows], v_s[h, :, rows]
        qh, ql = hi_lo(q_s[h, :, rows].astype(F32) * (SCALE * LOG2E))
        kk = jnp.concatenate([k_t, k_t], 0).T
        s = nn(kk, jnp.concatenate([qh, ql], 0))
        m = jnp.max(s, axis=0, keepdims=True)
        e = jnp.exp2(s - m).astype(BF16)
        e_s[u] = e
        o = nn(jnp.concatenate([v_t, jnp.ones((16, SEG), BF16)], 0), e)
        total = o[DH:DH + 1]
        r = 1.0 / total
        on_s[h, :, rows] = o[:DH] * r
        st_s[h, 0:1, rows] = r
        st_s[h, 1:2, rows] = m + jnp.log2(total)
        return carry

    lax.fori_loop(0, 2 * HEADS, near_forward, 0)

    for c in kv_in:
        c.wait_recv()
    kv_pair, kv_back = to_pair(kv_buf, 0)
    kv_pair.start()
    copies[3].wait()
    copies[4].wait()
    g_s[...] = nt(w_s[...], go_s[...]).astype(BF16).reshape(HEADS, DH, ROWS)
    kv_back.wait_recv()

    key_index = lanes(SPAN)

    def all_cols(buf, h, lo, hi):
        return jnp.concatenate([buf[n % 2, n // 2, h, lo:hi, :] for n in range(PEERS)], 1)

    def far_forward(h, carry):
        ph = phases[h]
        k_t, v_t = all_cols(kv_buf, h, 0, DH), all_cols(kv_buf, h, DH, 2 * DH)
        q_t = qd_buf[core, yx, h, 0:DH, :].astype(F32) * (SCALE * LOG2E)
        hi = q_t.astype(BF16).astype(F32)
        lhs = jnp.concatenate([hi, q_t - hi], 0).T.astype(BF16)
        s = nn(lhs, jnp.concatenate([k_t, k_t], 0))
        row = (key_index >> 5) * (RATE * BLK) + ph * BLK + (key_index & 31)
        s = jnp.where(row < valid[0], s, -1e30)
        m = jnp.max(s, axis=1, keepdims=True)
        e = jnp.exp2(s - m).astype(BF16)
        fe_s[h] = e
        o = nt(e, jnp.concatenate([v_t, jnp.ones((16, SPAN), BF16)], 0))
        total = o[:, DH:DH + 1]
        r = 1.0 / total
        packed = jnp.concatenate(
            [o[:, :DH] * r, jnp.broadcast_to(m + jnp.log2(total), (SUB, 32)), jnp.broadcast_to(r, (SUB, 32))], 1).T
        far_out, far_lse, far_r = packed[0:DH], packed[DH:DH + 1], packed[96:97]
        near_out = pick(lambda o: on_s[h, :, pl.ds(o, 128)], ph)
        near_lse = pick(lambda o: st_s[h, :, pl.ds(o, 128)], ph)[1:2]
        g = pick(lambda o: g_s[h, :, pl.ds(o, 128)], ph)
        mixing = 1.0 / (1.0 + jnp.exp2(near_lse - far_lse))
        rest = 1.0 / (1.0 + jnp.exp2(far_lse - near_lse))
        diff = far_out - near_out
        comb = near_out + mixing * diff
        far_dlse = jnp.sum(g * diff, axis=0, keepdims=True) * mixing * rest
        far_dout = (mixing * g).astype(BF16)
        fd = far_dout.astype(F32)
        term = far_dlse - jnp.sum(fd * far_out, axis=0, keepdims=True)
        qd_buf[core, yx, h, DH:2 * DH, :] = far_dout
        qd_buf[core, yx, h, 2 * DH:QD_ROWS, :] = jnp.concatenate(
            [*split3(-far_lse), *split3(term), jnp.zeros((10, SUB), BF16)], 0)
        scaled = (fd * far_r).astype(BF16).astype(F32)
        term_r = far_dlse * far_r - jnp.sum(scaled * far_out, axis=0, keepdims=True)
        fr_s[h, 0:DH, :] = scaled
        fr_s[h, DH:DH + 8, :] = jnp.broadcast_to(term_r, (8, SUB))
        stack = jnp.concatenate([comb, rest, -far_dlse, jnp.zeros((6, SUB), F32)], 0)
        parts = place_parts(stack, ph)
        for c in range(16):
            cols = pl.ds(c * 128, 128)
            mask = place_mask(ph, c)
            part = parts[c // 4]
            near = on_s[h, :, cols]
            at_s[h, :, cols] = jnp.where(mask, part[:DH], near).astype(BF16)
            factor = jnp.where(mask, part[DH:DH + 1], 1.0)
            dlse = jnp.where(mask, part[DH + 1:DH + 2], 0.0)
            rr = st_s[h, 0:1, cols]
            nd = (g_s[h, :, cols].astype(F32) * factor).astype(BF16).astype(F32)
            nd = (nd * rr).astype(BF16)
            nd_s[h, :, cols] = nd
            st_s[h, 2:3, cols] = dlse * rr - jnp.sum(nd.astype(F32) * near, axis=0, keepdims=True)
        return carry

    lax.fori_loop(0, HEADS, far_forward, 0)

    for c in kv_out:
        c.wait_send()
    kv_pair.wait_send()
    qd_out, qd_in = gather(qd_buf, qd_send, qd_recv)
    for c in qd_out:
        c.start()

    gw_s[...] = nn(at_s[...].reshape(HEADS * DH, ROWS), go_s[...])
    half = HEADS * DH // 2
    a_send[...] = gw_s[pl.ds(pl.multiple_of((1 - core) * half, 32), half), :].astype(BF16)
    a_copy = pltpu.make_async_remote_copy(a_send, a_recv, a_sem.at[0], a_sem.at[1], device_id=sibling, device_id_type=MESH)
    a_copy.start()

    def far_backward_q(h, carry):
        k_t, v_t = all_cols(kv_buf, h, 0, DH), all_cols(kv_buf, h, DH, 2 * DH)
        d = fr_s[h]
        term = d[DH:DH + 1]
        term_hi = term.astype(BF16).astype(F32)
        left = jnp.concatenate([d[:DH], term_hi, term - term_hi, jnp.zeros((62, SUB), F32)], 0).T.astype(BF16)
        ones = jnp.concatenate([jnp.ones((2, SPAN), BF16), jnp.zeros((62, SPAN), BF16)], 0)
        dprob = nn(left, jnp.concatenate([v_t, ones], 0))
        dscore = dprob.astype(BF16) * fe_s[h]
        fq_s[h] = nt(dscore, k_t).T * SCALE
        return carry

    lax.fori_loop(0, HEADS, far_backward_q, 0)

    quarter, wide = half // 2, D // 2
    b_out, b_in = [], []
    for k in range(1, 4):
        b_out.append(pltpu.make_async_remote_copy(
            b_send.at[(x + k) % 4], b_recv.at[x], b_ss.at[k - 1], b_rs.at[k - 1],
            device_id=same_core[k - 1], device_id_type=MESH))
        b_in.append(pltpu.make_async_remote_copy(
            b_send.at[(x + k) % 4], b_recv.at[(x + 4 - k) % 4], b_ss.at[k - 1], b_rs.at[k - 1],
            device_id=same_core[k - 1], device_id_type=MESH))
    c_out, c_in = [], []
    for k in range(1, 4):
        c_out.append(pltpu.make_async_remote_copy(
            c_buf.at[yg], c_buf.at[yg], c_ss.at[k - 1], c_rs.at[k - 1], device_id=y_peers[k - 1], device_id_type=MESH))
        there = (yg + 4 - k) % 4
        c_in.append(pltpu.make_async_remote_copy(
            c_buf.at[there], c_buf.at[there], c_ss.at[k - 1], c_rs.at[k - 1], device_id=y_peers[k - 1], device_id_type=MESH))
    d_out, d_in = [], []
    d_peers = [same_core[k - 1] for k in range(1, 4)] + [sibling] + other_core
    for k in range(1, 8):
        here = d_buf.at[core, x]
        d_out.append(pltpu.make_async_remote_copy(
            here, here, d_ss.at[k - 1], d_rs.at[k - 1], device_id=d_peers[k - 1], device_id_type=MESH))
        theirs = d_buf.at[core if k < 4 else 1 - core, (x + 4 - k % 4) % 4]
        d_in.append(pltpu.make_async_remote_copy(
            theirs, theirs, d_ss.at[k - 1], d_rs.at[k - 1], device_id=d_peers[k - 1], device_id_type=MESH))
    qd_pair, qd_back = to_pair(qd_buf, 1)

    def near_backward(u, carry):
        h, off = u // 2, pl.multiple_of((u % 2) * SEG, SEG)
        rows = pl.ds(off, SEG)
        q_t, k_t, v_t, gh = q_s[h, :, rows], k_s[h, :, rows], v_s[h, :, rows], nd_s[h, :, rows]
        th, tl = hi_lo(st_s[h, 2:3, rows])
        gg = jnp.concatenate([gh, jnp.concatenate([th, tl, jnp.zeros((14, SEG), BF16)], 0)], 0)
        vv = jnp.concatenate([v_t, jnp.ones((2, SEG), BF16), jnp.zeros((14, SEG), BF16)], 0).T
        for ib in range(2):
            cols = slice(ib * 512, ib * 512 + 512)
            dprob = nn(vv, gg[:, cols])
            ds = dprob.astype(BF16) * e_s[u, :, cols]
            ds_s[:, cols] = ds
            aq_s[h, :, pl.ds(pl.multiple_of(off + ib * 512, 512), 512)] = nn(k_t, ds) * SCALE
        for jb in range(2):
            cols = slice(jb * 512, jb * 512 + 512)
            out_cols = pl.ds(pl.multiple_of(off + jb * 512, 512), 512)
            ak_s[h, :, out_cols] = nt(ds_s[cols, :], q_t).T * SCALE
            av_s[h, :, out_cols] = nt(e_s[u, cols, :], gh).T

        @pl.when(u == 0)
        def _():
            a_copy.wait()
            mine = gw_s[pl.ds(pl.multiple_of(core * half, 32), half), :]
            half_s[...] = mine + a_recv[...].astype(F32)
            for t in range(4):
                b_send[t] = half_s[(t // 2) * quarter:(t // 2 + 1) * quarter, (t % 2) * wide:(t % 2 + 1) * wide].astype(BF16)
            for c in b_out:
                c.start()

        @pl.when(u == 2)
        def _():
            for c in b_in:
                c.wait_recv()
            b_recv[x] = b_send[x]
            total = b_recv[0].astype(F32)
            for t in range(1, 4):
                total = total + b_recv[t].astype(F32)
            c_buf[yg] = total.astype(BF16)
            for c in c_out:
                c.start()

        @pl.when(u == 3)
        def _():
            for c in c_in:
                c.wait_recv()
            total = c_buf[0].astype(F32)
            for t in range(1, 4):
                total = total + c_buf[t].astype(F32)
            d_buf[core, x] = total.astype(BF16)
            for c in d_out:
                c.start()

        @pl.when(u == 4)
        def _():
            for c in qd_in:
                c.wait_recv()
            qd_pair.start()

        return carry

    lax.fori_loop(0, 2 * HEADS, near_backward, 0)
    qd_back.wait_recv()

    def outs(h):
        return [
            pltpu.make_async_copy(oq_s.at[h], dq_hbm.at[0, h], out_sem.at[0, h]),
            pltpu.make_async_copy(ok_s.at[h], dk_hbm.at[0, h], out_sem.at[1, h]),
            pltpu.make_async_copy(ov_s.at[h], dv_hbm.at[0, h], out_sem.at[2, h]),
        ]

    def far_backward_kv(h, carry):
        ph = phases[h]
        q_t, do_t = all_cols(qd_buf, h, 0, DH), all_cols(qd_buf, h, DH, 2 * DH)
        stats = all_cols(qd_buf, h, 2 * DH, QD_ROWS)
        own_k = kv_buf[core, yx, h, 0:DH, :].astype(F32) * (SCALE * LOG2E)
        own_v = kv_buf[core, yx, h, DH:2 * DH, :].astype(F32)
        hi = own_k.astype(BF16).astype(F32)
        index = lax.broadcasted_iota(jnp.int32, (16, SUB), 0)
        first = jnp.where(index < 3, 1.0, 0.0)
        second = jnp.where((index >= 3) & (index < 6), 1.0, 0.0)
        zeros = jnp.zeros((48, SUB), F32)
        left_s = jnp.concatenate([hi, own_k - hi, first, zeros, zeros, jnp.zeros((16, SUB), F32)], 0).T.astype(BF16)
        s = nn(left_s[:, :QD_ROWS], jnp.concatenate([q_t, q_t, stats], 0))
        j = lax.broadcasted_iota(jnp.int32, (SUB, 1), 0)
        row = sq * ROWS + (j >> 5) * (RATE * BLK) + ph * BLK + (j & 31)
        probs = jnp.where(row < valid[0], jnp.exp2(s), 0.0).astype(BF16)
        left_d = jnp.concatenate([own_v, second, zeros], 0).T.astype(BF16)
        dprob = nn(left_d[:, :DH + 16], jnp.concatenate([do_t, stats], 0))
        dscore = dprob.astype(BF16) * probs
        both = jnp.concatenate([nt(dscore, q_t) * SCALE, nt(probs, do_t)], 1).T
        parts_k, parts_v = place_parts(both[:DH], ph), place_parts(both[DH:], ph)
        parts_q = place_parts(fq_s[h], ph)
        for c in range(16):
            cols = pl.ds(c * 128, 128)
            mask = place_mask(ph, c)
            for out, near, parts in ((oq_s, aq_s, parts_q), (ok_s, ak_s, parts_k), (ov_s, av_s, parts_v)):
                out[h, :, cols] = (near[h, :, cols] + jnp.where(mask, parts[c // 4], 0.0)).astype(BF16)
        for c in outs(h):
            c.start()
        return carry

    lax.fori_loop(0, HEADS, far_backward_kv, 0)

    for c in d_in:
        c.wait_recv()
    for cc in range(2):
        for t in range(4):
            gw_s[cc * half + (t // 2) * quarter:cc * half + (t // 2 + 1) * quarter, (t % 2) * wide:(t % 2 + 1) * wide] = (
                d_buf[cc, t].astype(F32))
    gw_copy = pltpu.make_async_copy(gw_s, gw_hbm, in_sem.at[0])
    gw_copy.start()
    for c in qd_out + [qd_pair] + b_out + c_out + d_out:
        c.wait_send()
    for h in range(HEADS):
        for c in outs(h):
            c.wait()
    gw_copy.wait()


def shards(queries, key_states, value_states, out_weight, grad_output, phases, valid_rows):
    big = lambda dtype: pltpu.VMEM((HEADS, DH, ROWS), dtype)
    dma = pltpu.SemaphoreType.DMA
    any_spec = pl.BlockSpec(memory_space=pl.ANY)
    smem = pl.BlockSpec(memory_space=pltpu.SMEM)
    chunk = (HEADS * DH // 4, D // 2)
    state = jax.ShapeDtypeStruct(queries.shape, BF16)
    return pl.pallas_call(
        kernel,
        out_shape=[state, state, state, jax.ShapeDtypeStruct((HEADS * DH, D), F32)],
        in_specs=[smem, smem] + [any_spec] * 5,
        out_specs=[any_spec] * 4,
        scratch_shapes=[
            big(BF16), big(BF16), big(BF16),
            pltpu.VMEM((HEADS * DH, D), BF16), pltpu.VMEM((ROWS, D), BF16),
            big(BF16),
            pltpu.VMEM((2 * HEADS, SEG, SEG), BF16), pltpu.VMEM((SEG, SEG), BF16),
            big(F32), pltpu.VMEM((HEADS, 8, ROWS), F32), big(BF16), big(BF16),
            pltpu.VMEM((2, 8, HEADS, 2 * DH, SUB), BF16), pltpu.VMEM((2, 8, HEADS, QD_ROWS, SUB), BF16),
            pltpu.VMEM((HEADS, SUB, SPAN), BF16), pltpu.VMEM((HEADS, DH, SUB), F32), pltpu.VMEM((HEADS, DH + 8, SUB), F32),
            big(F32), big(F32), big(F32), big(BF16), big(BF16), big(BF16),
            pltpu.VMEM((HEADS * DH, D), F32),
            pltpu.VMEM((HEADS * DH // 2, D), BF16), pltpu.VMEM((HEADS * DH // 2, D), BF16),
            pltpu.VMEM((HEADS * DH // 2, D), F32),
            pltpu.VMEM((4, *chunk), BF16), pltpu.VMEM((4, *chunk), BF16), pltpu.VMEM((4, *chunk), BF16),
            pltpu.VMEM((2, 4, *chunk), BF16),
            dma((5,)), dma((3, HEADS)), dma((7,)), dma((7,)), dma((7,)), dma((7,)), dma((2,)), dma((2,)),
            dma((2,)), dma((3,)), dma((3,)), dma((3,)), dma((3,)), dma((7,)), dma((7,)),
        ],
        compiler_params=pltpu.CompilerParams(
            collective_id=0, has_side_effects=True, vmem_limit_bytes=58 << 20),
        name="dilated_backward",
    )(phases, valid_rows, queries, key_states, value_states, out_weight, grad_output)


def solution(mesh):
    heads = P("dp", "tensor", None, "seq")
    return jax.shard_map(
        shards, mesh=mesh,
        in_specs=(heads, heads, heads, P("tensor", None), P("dp", "seq", None), P("tensor"), P("dp")),
        out_specs=(heads, heads, heads, P("tensor", None)),
        check_vma=False,
    )
```

time: 407 us -> 60.8 us (0.15)
  local copies, waits for them, and re-layouts: 159 us -> 5.98 us
  other arithmetic: 104 us -> 0 us
  matrix products: 82.1 us -> 0 us
  Pallas kernels: 0 us -> 53.3 us
  blocking collectives: 42.2 us -> 0 us
  between operations: 16.4 us -> 1.31 us
    dot_general x14 -> x0, matrix products: 82.1 us -> none  [the longest x12 76.3 us: product(): return jnp.einsum(form, left, right, preferred_element_type=jnp.float32)]
    scatter x55 -> x0, local copies, waits for them, and re-layouts: 70 us -> none
    scatter x38 -> x0, other arithmetic: 69.4 us -> none
    pallas_call x0 -> x1, Pallas kernels: none -> 53.3 us  [shards(): pl.pallas_call(kernel, out_shape=[state, state, state, jax.ShapeDtypeStru...]
    all_gather x2 -> x0, blocking collectives: 42.2 us -> none  [the longest x1 23.4 us: shards(): lax.all_gather(key_pick, 'seq', axis=1, tiled=True)]
    reshape x18 -> x0, local copies, waits for them, and re-layouts: 39.8 us -> none  [the longest x4 13.1 us: select_rows(): blocks = matrix.reshape(row_count // (RATE * BLK), RATE, BLK, col_count)]
    gather x6 -> x0, local copies, waits for them, and re-layouts: 12.1 us -> none  [select_rows(): picked = lax.dynamic_index_in_dim(blocks, head_phase, 1, keepdims=False)]
    unnamed x45 -> x8, local copies, waits for them, and re-layouts: 17.7 us -> 5.98 us
  transfers between devices with their start and end apart: 3 -> 0, of which waited for: 0 -> 0; matrix products, arithmetic and copies ran while one was open for 50% -> 0% of each run, Pallas kernels for 0% -> 0%
where the time goes in v1:
time: 60.8 us; the launch traced here: 60.6 us
  Pallas kernels  53.3 us (88%)
  local copies, waits for them, and re-layouts  5.98 us (10%)
  between operations  1.31 us (2%)
    pallas_call x1, Pallas kernels, shards(): pl.pallas_call(kernel, out_shape=[state, state, state, jax.ShapeDtypeStru...  53.3 us
    unnamed x8, local copies, waits for them, and re-layouts  5.98 us

profile of v1, /device:TPU:1, one launch (start us, length us, event | category | flops | bytes accessed | tf_op | source)
XLA Modules:
  0.0 60.6 jit_solution(13152419855535147920)
XLA Ops:
  1.3 53.3 %dilated_backward.1 = (bf16[1,3,64,2048]{3,2,1,0:T(8,128)(2,1)}, bf16[1,3,64,2048]{3,2,1,0:T(8,128)(2,1)}, bf16[1,3,64,2048]{3,2,1,0:T(8,128)(2,1)}, f32[192,768]{1,0:T(8,128)}) custom-call(s32[3]{0:T(128)} %phases.1, s32[1]{0:T(128)S(6)} %copy.15.valid, bf16[1,3,64,2048]{3,2,1,0:T(8,128)(2,1)} %q_hbm.1, bf16[1,3,64,2048]{3,2,1,0:T(8,128)(2,1)} %k_hbm.1, ...), custom_call_target="tpu_custom_call" | custom-call | tf_op jit(solution)/shard_map/dilated_backward/pallas_call | solution.py:434
  54.6 0.0 copy-start
  54.6 0.0 copy-start.1
  54.6 2.2 %copy.16 = bf16[1,3,64,2048]{3,2,1,0:T(8,128)(2,1)} copy(bf16[1,3,64,2048]{3,2,1,0:T(8,128)(2,1)} %get-tuple-element.8) | data formatting | bytes 1572864
  56.8 2.1 %copy.17 = bf16[1,3,64,2048]{3,2,1,0:T(8,128)(2,1)} copy(bf16[1,3,64,2048]{3,2,1,0:T(8,128)(2,1)} %get-tuple-element.9) | data formatting | bytes 1572864
  58.9 0.0 copy-done
  58.9 0.9 %copy.18 = bf16[1,3,64,2048]{3,2,1,0:T(8,128)(2,1)} copy(bf16[1,3,64,2048]{3,2,1,0:T(8,128)(2,1)S(1)} %copy-done) | data formatting | bytes 1572864
  59.8 0.0 copy-done.1
  59.8 0.8 %copy.19 = f32[192,768]{1,0:T(8,128)} copy(f32[192,768]{1,0:T(8,128)S(1)} %copy-done.1) | data formatting | bytes 1179648
Async XLA Ops:
  54.6 4.3 %copy-start = (bf16[1,3,64,2048]{3,2,1,0:T(8,128)(2,1)S(1)}, bf16[1,3,64,2048]{3,2,1,0:T(8,128)(2,1)}, u32[]{:S(2)}) copy-start(bf16[1,3,64,2048]{3,2,1,0:T(8,128)(2,1)} %get-tuple-element.10) | copy-start | bytes 2359300
  54.6 5.2 %copy-start.1 = (f32[192,768]{1,0:T(8,128)S(1)}, f32[192,768]{1,0:T(8,128)}, u32[]{:S(2)}) copy-start(f32[192,768]{1,0:T(8,128)} %get-tuple-element.11) | copy-start | bytes 1769476

commit v2 on v1

--- a/solution.py
+++ b/solution.py
@@ -19,7 +19,8 @@
 SPAN = PEERS * SUB
 SCALE = 0.125
 LOG2E = 1.4426950408889634
-QD_ROWS = 144
+DO_ROWS = 80
+QD_ROWS = DH + DO_ROWS
 MESH = pl.DeviceIdType.MESH
 
 
@@ -82,14 +83,13 @@
     return (lanes() >> 5) == want
 
 
-def kernel(
+def front_kernel(
     phases, valid, q_hbm, k_hbm, v_hbm, w_hbm, go_hbm,
-    dq_hbm, dk_hbm, dv_hbm, gw_hbm,
+    aq_hbm, ak_hbm, av_hbm, fq_hbm, own_hbm, q_far, do_far, d_far,
     q_s, k_s, v_s, w_s, go_s, g_s, e_s, ds_s, on_s, st_s, nd_s, at_s,
-    kv_buf, qd_buf, fe_s, fq_s, fr_s,
-    aq_s, ak_s, av_s, oq_s, ok_s, ov_s,
-    gw_s, a_send, a_recv, half_s, b_send, b_recv, c_buf, d_buf,
-    in_sem, out_sem, kv_send, kv_recv, qd_send, qd_recv, pair_send, pair_recv,
+    kv_buf, q_own, do_own, fe_s, fq_s, fr_s, aq_s, ak_s, av_s,
+    gw_s, a_send, a_recv, half_s, b_send, b_recv, c_buf, d_own,
+    in_sem, out_sem, own_sem, kv_send, kv_recv, qd_send, qd_recv, pair_send, pair_recv,
     a_sem, b_ss, b_rs, c_ss, c_rs, d_ss, d_rs,
 ):
     dp, sq, tz = lax.axis_index("dp"), lax.axis_index("seq"), lax.axis_index("tensor")
@@ -132,35 +132,49 @@
         c.wait()
     for h in range(HEADS):
         ph = phases[h]
-        kv_buf[core, yx, h, 0:DH, :] = pick(lambda o: k_s[h, :, pl.ds(o, 128)], ph).astype(BF16)
-        kv_buf[core, yx, h, DH:2 * DH, :] = pick(lambda o: v_s[h, :, pl.ds(o, 128)], ph).astype(BF16)
+        kv_buf[core, h, yx, 0:DH, :] = pick(lambda o: k_s[h, :, pl.ds(o, 128)], ph).astype(BF16)
+        kv_buf[core, h, yx, DH:2 * DH, :] = pick(lambda o: v_s[h, :, pl.ds(o, 128)], ph).astype(BF16)
     pl.semaphore_wait(barrier, len(greet))
 
-    def gather(buf, ss, rs):
+    def gather(mine, slot, ss, rs, base):
         sends, recvs = [], []
         for k in range(1, 8):
-            mine = buf.at[core, yx]
+            n = base + k - 1
             sends.append(pltpu.make_async_remote_copy(
-                mine, mine, ss.at[k - 1], rs.at[k - 1], device_id=same_core[k - 1], device_id_type=MESH))
-            theirs = buf.at[core, from_yx(k)]
+                mine, slot(yx), ss.at[n], rs.at[n], device_id=same_core[k - 1], device_id_type=MESH))
             recvs.append(pltpu.make_async_remote_copy(
-                theirs, theirs, ss.at[k - 1], rs.at[k - 1], device_id=same_core[k - 1], device_id_type=MESH))
+                mine, slot(from_yx(k)), ss.at[n], rs.at[n], device_id=same_core[k - 1], device_id_type=MESH))
         return sends, recvs
 
     def to_pair(buf, i):
         out = pltpu.make_async_remote_copy(
-            buf.at[core], buf.at[core], pair_send.at[i], pair_recv.at[i], device_id=sibling, device_id_type=MESH)
+            buf(core), buf(core), pair_send.at[i], pair_recv.at[i], device_id=sibling, device_id_type=MESH)
         back = pltpu.make_async_remote_copy(
-            buf.at[1 - core], buf.at[1 - core], pair_send.at[i], pair_recv.at[i], device_id=sibling, device_id_type=MESH)
+            buf(1 - core), buf(1 - core), pair_send.at[i], pair_recv.at[i], device_id=sibling, device_id_type=MESH)
         return out, back
 
-    kv_out, kv_in = gather(kv_buf, kv_send, kv_recv)
-    for c in kv_out:
+    kv_out, kv_in, kv_pair = [], [], []
+    for h in range(HEADS):
+        sends, recvs = gather(kv_buf.at[core, h, yx], lambda n, h=h: kv_buf.at[core, h, n], kv_send, kv_recv, 7 * h)
+        kv_out.append(sends)
+        kv_in.append(recvs)
+        kv_pair.append(to_pair(lambda c, h=h: kv_buf.at[c, h], h))
+        for c in sends:
+            c.start()
+
+    copies[2].wait()
+    for h in range(HEADS):
+        q_own[h] = pick(lambda o: q_s[h, :, pl.ds(o, 128)], phases[h]).astype(BF16)
+    own_copies = [
+        pltpu.make_async_copy(kv_buf.at[core, h, yx], own_hbm.at[h], own_sem.at[h]) for h in range(HEADS)]
+    own_copies.append(pltpu.make_async_copy(q_own, q_far.at[core, yx], own_sem.at[3]))
+    for c in own_copies:
         c.start()
 
-    copies[2].wait()
-    for h in range(HEADS):
-        qd_buf[core, yx, h, 0:DH, :] = pick(lambda o: q_s[h, :, pl.ds(o, 128)], phases[h]).astype(BF16)
+    def forward_pair(h):
+        for c in kv_in[h]:
+            c.wait_recv()
+        kv_pair[h][0].start()
 
     def near_forward(u, carry):
         h, off = u // 2, pl.multiple_of((u % 2) * SEG, SEG)
@@ -180,26 +194,29 @@
         st_s[h, 1:2, rows] = m + jnp.log2(total)
         return carry
 
-    lax.fori_loop(0, 2 * HEADS, near_forward, 0)
-
-    for c in kv_in:
-        c.wait_recv()
-    kv_pair, kv_back = to_pair(kv_buf, 0)
-    kv_pair.start()
+    for u in range(2 * HEADS):
+        near_forward(u, 0)
+        if u == 3:
+            forward_pair(0)
+    forward_pair(1)
     copies[3].wait()
     copies[4].wait()
     g_s[...] = nt(w_s[...], go_s[...]).astype(BF16).reshape(HEADS, DH, ROWS)
-    kv_back.wait_recv()
+    forward_pair(2)
+    q_out, q_in = gather(q_own, lambda n: q_far.at[core, n], qd_send, qd_recv, 0)
+    q_pair = to_pair(lambda c: q_far.at[c], HEADS)
+    for c in q_out:
+        c.start()
 
     key_index = lanes(SPAN)
 
     def all_cols(buf, h, lo, hi):
-        return jnp.concatenate([buf[n % 2, n // 2, h, lo:hi, :] for n in range(PEERS)], 1)
+        return jnp.concatenate([buf[n % 2, h, n // 2, lo:hi, :] for n in range(PEERS)], 1)
 
     def far_forward(h, carry):
         ph = phases[h]
         k_t, v_t = all_cols(kv_buf, h, 0, DH), all_cols(kv_buf, h, DH, 2 * DH)
-        q_t = qd_buf[core, yx, h, 0:DH, :].astype(F32) * (SCALE * LOG2E)
+        q_t = q_own[h].astype(F32) * (SCALE * LOG2E)
         hi = q_t.astype(BF16).astype(F32)
         lhs = jnp.concatenate([hi, q_t - hi], 0).T.astype(BF16)
         s = nn(lhs, jnp.concatenate([k_t, k_t], 0))
@@ -225,8 +242,8 @@
         far_dout = (mixing * g).astype(BF16)
         fd = far_dout.astype(F32)
         term = far_dlse - jnp.sum(fd * far_out, axis=0, keepdims=True)
-        qd_buf[core, yx, h, DH:2 * DH, :] = far_dout
-        qd_buf[core, yx, h, 2 * DH:QD_ROWS, :] = jnp.concatenate(
+        do_own[h, 0:DH, :] = far_dout
+        do_own[h, DH:DO_ROWS, :] = jnp.concatenate(
             [*split3(-far_lse), *split3(term), jnp.zeros((10, SUB), BF16)], 0)
         scaled = (fd * far_r).astype(BF16).astype(F32)
         term_r = far_dlse * far_r - jnp.sum(scaled * far_out, axis=0, keepdims=True)
@@ -249,14 +266,17 @@
             st_s[h, 2:3, cols] = dlse * rr - jnp.sum(nd.astype(F32) * near, axis=0, keepdims=True)
         return carry
 
-    lax.fori_loop(0, HEADS, far_forward, 0)
-
-    for c in kv_out:
-        c.wait_send()
-    kv_pair.wait_send()
-    qd_out, qd_in = gather(qd_buf, qd_send, qd_recv)
-    for c in qd_out:
+    for h in range(HEADS):
+        kv_pair[h][1].wait_recv()
+    for h in range(HEADS):
+        far_forward(h, 0)
+
+    do_out, do_in = gather(do_own, lambda n: do_far.at[core, n], qd_send, qd_recv, 7)
+    do_pair = to_pair(lambda c: do_far.at[c], HEADS + 1)
+    for c in do_out:
         c.start()
+    do_copy = pltpu.make_async_copy(do_own, do_far.at[core, yx], own_sem.at[4])
+    do_copy.start()
 
     gw_s[...] = nn(at_s[...].reshape(HEADS * DH, ROWS), go_s[...])
     half = HEADS * DH // 2
@@ -276,7 +296,10 @@
         fq_s[h] = nt(dscore, k_t).T * SCALE
         return carry
 
-    lax.fori_loop(0, HEADS, far_backward_q, 0)
+    for h in range(HEADS):
+        far_backward_q(h, 0)
+    fq_copy = pltpu.make_async_copy(fq_s, fq_hbm, own_sem.at[5])
+    fq_copy.start()
 
     quarter, wide = half // 2, D // 2
     b_out, b_in = [], []
@@ -297,13 +320,20 @@
     d_out, d_in = [], []
     d_peers = [same_core[k - 1] for k in range(1, 4)] + [sibling] + other_core
     for k in range(1, 8):
-        here = d_buf.at[core, x]
         d_out.append(pltpu.make_async_remote_copy(
-            here, here, d_ss.at[k - 1], d_rs.at[k - 1], device_id=d_peers[k - 1], device_id_type=MESH))
-        theirs = d_buf.at[core if k < 4 else 1 - core, (x + 4 - k % 4) % 4]
+            d_own, d_far.at[core, x], d_ss.at[k - 1], d_rs.at[k - 1], device_id=d_peers[k - 1], device_id_type=MESH))
+        theirs = d_far.at[core if k < 4 else 1 - core, (x + 4 - k % 4) % 4]
         d_in.append(pltpu.make_async_remote_copy(
-            theirs, theirs, d_ss.at[k - 1], d_rs.at[k - 1], device_id=d_peers[k - 1], device_id_type=MESH))
-    qd_pair, qd_back = to_pair(qd_buf, 1)
+            d_own, theirs, d_ss.at[k - 1], d_rs.at[k - 1], device_id=d_peers[k - 1], device_id_type=MESH))
+    d_copy = pltpu.make_async_copy(d_own, d_far.at[core, x], own_sem.at[6])
+
+    def outs(h):
+        return [
+            pltpu.make_async_copy(aq_s.at[h], aq_hbm.at[h], out_sem.at[0, h]),
+            pltpu.make_async_copy(ak_s.at[h], ak_hbm.at[h], out_sem.at[1, h]),
+            pltpu.make_async_copy(av_s.at[h], av_hbm.at[h], out_sem.at[2, h]),
+        ]
+
 
     def near_backward(u, carry):
         h, off = u // 2, pl.multiple_of((u % 2) * SEG, SEG)
@@ -317,15 +347,25 @@
             dprob = nn(vv, gg[:, cols])
             ds = dprob.astype(BF16) * e_s[u, :, cols]
             ds_s[:, cols] = ds
-            aq_s[h, :, pl.ds(pl.multiple_of(off + ib * 512, 512), 512)] = nn(k_t, ds) * SCALE
+            aq_s[h, :, pl.ds(pl.multiple_of(off + ib * 512, 512), 512)] = (nn(k_t, ds) * SCALE).astype(BF16)
         for jb in range(2):
             cols = slice(jb * 512, jb * 512 + 512)
             out_cols = pl.ds(pl.multiple_of(off + jb * 512, 512), 512)
-            ak_s[h, :, out_cols] = nt(ds_s[cols, :], q_t).T * SCALE
-            av_s[h, :, out_cols] = nt(e_s[u, cols, :], gh).T
+            ak_s[h, :, out_cols] = (nt(ds_s[cols, :], q_t).T * SCALE).astype(BF16)
+            av_s[h, :, out_cols] = nt(e_s[u, cols, :], gh).T.astype(BF16)
+
+        @pl.when(u % 2 == 1)
+        def _():
+            for c in outs(h):
+                c.start()
 
         @pl.when(u == 0)
         def _():
+            for c in own_copies:
+                c.wait()
+            for c in q_in:
+                c.wait_recv()
+            q_pair[0].start()
             a_copy.wait()
             mine = gw_s[pl.ds(pl.multiple_of(core * half, 32), half), :]
             half_s[...] = mine + a_recv[...].astype(F32)
@@ -334,7 +374,7 @@
             for c in b_out:
                 c.start()
 
-        @pl.when(u == 2)
+        @pl.when(u == 3)
         def _():
             for c in b_in:
                 c.wait_recv()
@@ -346,41 +386,64 @@
             for c in c_out:
                 c.start()
 
-        @pl.when(u == 3)
+        @pl.when(u == 4)
         def _():
+            for c in do_in:
+                c.wait_recv()
+            do_copy.wait()
+            do_pair[0].start()
             for c in c_in:
                 c.wait_recv()
             total = c_buf[0].astype(F32)
             for t in range(1, 4):
                 total = total + c_buf[t].astype(F32)
-            d_buf[core, x] = total.astype(BF16)
+            d_own[...] = total.astype(BF16)
             for c in d_out:
                 c.start()
-
-        @pl.when(u == 4)
-        def _():
-            for c in qd_in:
-                c.wait_recv()
-            qd_pair.start()
+            d_copy.start()
 
         return carry
 
     lax.fori_loop(0, 2 * HEADS, near_backward, 0)
-    qd_back.wait_recv()
-
-    def outs(h):
-        return [
-            pltpu.make_async_copy(oq_s.at[h], dq_hbm.at[0, h], out_sem.at[0, h]),
-            pltpu.make_async_copy(ok_s.at[h], dk_hbm.at[0, h], out_sem.at[1, h]),
-            pltpu.make_async_copy(ov_s.at[h], dv_hbm.at[0, h], out_sem.at[2, h]),
-        ]
-
-    def far_backward_kv(h, carry):
+    fq_copy.wait()
+    d_copy.wait()
+    for sends in kv_out:
+        for c in sends:
+            c.wait_send()
+    for pair in kv_pair + [q_pair, do_pair]:
+        pair[0].wait_send()
+    for c in q_out + do_out + b_out + c_out + d_out:
+        c.wait_send()
+    q_pair[1].wait_recv()
+    do_pair[1].wait_recv()
+    for c in d_in:
+        c.wait_recv()
+    for h in range(HEADS):
+        for c in outs(h):
+            c.wait()
+
+
+def back_kernel(
+    phases, valid, aq_hbm, ak_hbm, av_hbm, fq_hbm, own_hbm, q_far, do_far, d_far,
+    dq_hbm, dk_hbm, dv_hbm, gw_hbm,
+    aq_s, ak_s, av_s, fq_s, own_s, q_buf, do_buf, d_buf, oq_s, ok_s, ov_s, gw_s, in_sem, out_sem,
+):
+    sq = lax.axis_index("seq")
+    pairs = ((q_far, q_buf), (own_hbm, own_s), (do_far, do_buf), (fq_hbm, fq_s),
+             (aq_hbm, aq_s), (ak_hbm, ak_s), (av_hbm, av_s), (d_far, d_buf))
+    copies = [pltpu.make_async_copy(a, b, in_sem.at[n]) for n, (a, b) in enumerate(pairs)]
+    for c in copies:
+        c.start()
+
+    def all_cols(buf, h, lo, hi):
+        return jnp.concatenate([buf[n % 2, n // 2, h, lo:hi, :] for n in range(PEERS)], 1)
+
+    def far_backward_kv(h):
         ph = phases[h]
-        q_t, do_t = all_cols(qd_buf, h, 0, DH), all_cols(qd_buf, h, DH, 2 * DH)
-        stats = all_cols(qd_buf, h, 2 * DH, QD_ROWS)
-        own_k = kv_buf[core, yx, h, 0:DH, :].astype(F32) * (SCALE * LOG2E)
-        own_v = kv_buf[core, yx, h, DH:2 * DH, :].astype(F32)
+        q_t, do_t = all_cols(q_buf, h, 0, DH), all_cols(do_buf, h, 0, DH)
+        stats = all_cols(do_buf, h, DH, DO_ROWS)
+        own_k = own_s[h, 0:DH, :].astype(F32) * (SCALE * LOG2E)
+        own_v = own_s[h, DH:2 * DH, :].astype(F32)
         hi = own_k.astype(BF16).astype(F32)
         index = lax.broadcasted_iota(jnp.int32, (16, SUB), 0)
         first = jnp.where(index < 3, 1.0, 0.0)
@@ -394,34 +457,35 @@
         left_d = jnp.concatenate([own_v, second, zeros], 0).T.astype(BF16)
         dprob = nn(left_d[:, :DH + 16], jnp.concatenate([do_t, stats], 0))
         dscore = dprob.astype(BF16) * probs
-        both = jnp.concatenate([nt(dscore, q_t) * SCALE, nt(probs, do_t)], 1).T
-        parts_k, parts_v = place_parts(both[:DH], ph), place_parts(both[DH:], ph)
+        return jnp.concatenate([nt(dscore, q_t) * SCALE, nt(probs, do_t)], 1).T
+
+    for c in copies[:3]:
+        c.wait()
+    both = [far_backward_kv(h) for h in range(HEADS)]
+    for c in copies[3:]:
+        c.wait()
+    outs = []
+    for h in range(HEADS):
+        ph = phases[h]
+        parts_k, parts_v = place_parts(both[h][:DH], ph), place_parts(both[h][DH:], ph)
         parts_q = place_parts(fq_s[h], ph)
         for c in range(16):
             cols = pl.ds(c * 128, 128)
             mask = place_mask(ph, c)
             for out, near, parts in ((oq_s, aq_s, parts_q), (ok_s, ak_s, parts_k), (ov_s, av_s, parts_v)):
-                out[h, :, cols] = (near[h, :, cols] + jnp.where(mask, parts[c // 4], 0.0)).astype(BF16)
-        for c in outs(h):
-            c.start()
-        return carry
-
-    lax.fori_loop(0, HEADS, far_backward_kv, 0)
-
-    for c in d_in:
-        c.wait_recv()
+                out[h, :, cols] = (near[h, :, cols].astype(F32) + jnp.where(mask, parts[c // 4], 0.0)).astype(BF16)
+        for n, (a, b) in enumerate(((oq_s, dq_hbm), (ok_s, dk_hbm), (ov_s, dv_hbm))):
+            outs.append(pltpu.make_async_copy(a.at[h], b.at[0, h], out_sem.at[n, h]))
+            outs[-1].start()
+    half, quarter, wide = HEADS * DH // 2, HEADS * DH // 4, D // 2
     for cc in range(2):
         for t in range(4):
             gw_s[cc * half + (t // 2) * quarter:cc * half + (t // 2 + 1) * quarter, (t % 2) * wide:(t % 2 + 1) * wide] = (
                 d_buf[cc, t].astype(F32))
-    gw_copy = pltpu.make_async_copy(gw_s, gw_hbm, in_sem.at[0])
-    gw_copy.start()
-    for c in qd_out + [qd_pair] + b_out + c_out + d_out:
-        c.wait_send()
-    for h in range(HEADS):
-        for c in outs(h):
-            c.wait()
-    gw_copy.wait()
+    outs.append(pltpu.make_async_copy(gw_s, gw_hbm, out_sem.at[3, 0]))
+    outs[-1].start()
+    for c in outs:
+        c.wait()
 
 
 def shards(queries, key_states, value_states, out_weight, grad_output, phases, valid_rows):
@@ -431,32 +495,48 @@
     smem = pl.BlockSpec(memory_space=pltpu.SMEM)
     chunk = (HEADS * DH // 4, D // 2)
     state = jax.ShapeDtypeStruct(queries.shape, BF16)
-    return pl.pallas_call(
-        kernel,
-        out_shape=[state, state, state, jax.ShapeDtypeStruct((HEADS * DH, D), F32)],
+    near = jax.ShapeDtypeStruct((HEADS, DH, ROWS), BF16)
+    shape = jax.ShapeDtypeStruct
+    passed = [
+        near, near, near, shape((HEADS, DH, SUB), F32), shape((HEADS, 2 * DH, SUB), BF16),
+        shape((2, 8, HEADS, DH, SUB), BF16), shape((2, 8, HEADS, DO_ROWS, SUB), BF16), shape((2, 4, *chunk), BF16)]
+    between = pl.pallas_call(
+        front_kernel,
+        out_shape=passed,
         in_specs=[smem, smem] + [any_spec] * 5,
-        out_specs=[any_spec] * 4,
+        out_specs=[any_spec] * 8,
         scratch_shapes=[
             big(BF16), big(BF16), big(BF16),
             pltpu.VMEM((HEADS * DH, D), BF16), pltpu.VMEM((ROWS, D), BF16),
             big(BF16),
             pltpu.VMEM((2 * HEADS, SEG, SEG), BF16), pltpu.VMEM((SEG, SEG), BF16),
             big(F32), pltpu.VMEM((HEADS, 8, ROWS), F32), big(BF16), big(BF16),
-            pltpu.VMEM((2, 8, HEADS, 2 * DH, SUB), BF16), pltpu.VMEM((2, 8, HEADS, QD_ROWS, SUB), BF16),
+            pltpu.VMEM((2, HEADS, 8, 2 * DH, SUB), BF16),
+            pltpu.VMEM((HEADS, DH, SUB), BF16), pltpu.VMEM((HEADS, DO_ROWS, SUB), BF16),
             pltpu.VMEM((HEADS, SUB, SPAN), BF16), pltpu.VMEM((HEADS, DH, SUB), F32), pltpu.VMEM((HEADS, DH + 8, SUB), F32),
-            big(F32), big(F32), big(F32), big(BF16), big(BF16), big(BF16),
+            big(BF16), big(BF16), big(BF16),
             pltpu.VMEM((HEADS * DH, D), F32),
             pltpu.VMEM((HEADS * DH // 2, D), BF16), pltpu.VMEM((HEADS * DH // 2, D), BF16),
             pltpu.VMEM((HEADS * DH // 2, D), F32),
             pltpu.VMEM((4, *chunk), BF16), pltpu.VMEM((4, *chunk), BF16), pltpu.VMEM((4, *chunk), BF16),
-            pltpu.VMEM((2, 4, *chunk), BF16),
-            dma((5,)), dma((3, HEADS)), dma((7,)), dma((7,)), dma((7,)), dma((7,)), dma((2,)), dma((2,)),
+            pltpu.VMEM(chunk, BF16),
+            dma((5,)), dma((3, HEADS)), dma((7,)), dma((21,)), dma((21,)), dma((14,)), dma((14,)), dma((5,)), dma((5,)),
             dma((2,)), dma((3,)), dma((3,)), dma((3,)), dma((3,)), dma((7,)), dma((7,)),
         ],
         compiler_params=pltpu.CompilerParams(
             collective_id=0, has_side_effects=True, vmem_limit_bytes=58 << 20),
-        name="dilated_backward",
+        name="front",
     )(phases, valid_rows, queries, key_states, value_states, out_weight, grad_output)
+    return pl.pallas_call(
+        back_kernel,
+        out_shape=[state, state, state, shape((HEADS * DH, D), F32)],
+        in_specs=[smem, smem] + [any_spec] * 8,
+        out_specs=[any_spec] * 4,
+        scratch_shapes=[pltpu.VMEM(p.shape, p.dtype) for p in passed] + [
+            big(BF16), big(BF16), big(BF16), pltpu.VMEM((HEADS * DH, D), F32), dma((8,)), dma((4, HEADS))],
+        compiler_params=pltpu.CompilerParams(vmem_limit_bytes=58 << 20),
+        name="back",
+    )(phases, valid_rows, *between)
 
 
 def solution(mesh):

time: 60.8 us -> 52.6 us (0.87)
  local copies, waits for them, and re-layouts: 5.98 us -> 0 us
  Pallas kernels: 53.3 us -> 51 us
    unnamed x8 -> x0, local copies, waits for them, and re-layouts: 5.98 us -> none
    pallas_call x1 -> x2, Pallas kernels: 53.3 us -> 51 us  [the longest x1 44.7 us: shards(): pl.pallas_call(front_kernel, out_shape=passed, in_specs=[smem, smem] + [a...]
where the time goes in v2:
time: 52.6 us; the launch traced here: 52.4 us
  Pallas kernels  51 us (97%)
  between operations  1.45 us (3%)
    pallas_call x1, Pallas kernels, shards(): pl.pallas_call(front_kernel, out_shape=passed, in_specs=[smem, smem] + [a...  44.7 us
    pallas_call x1, Pallas kernels, shards(): pl.pallas_call(back_kernel, out_shape=[state, state, state, shape((HEADS...  6.28 us

profile of v2, /device:TPU:1, one launch (start us, length us, event | category | flops | bytes accessed | tf_op | source)
XLA Modules:
  0.0 52.4 jit_solution(16647587734298450751)
XLA Ops:
  1.3 44.7 %front.1 = (bf16[3,64,2048]{2,1,0:T(8,128)(2,1)}, bf16[3,64,2048]{2,1,0:T(8,128)(2,1)}, bf16[3,64,2048]{2,1,0:T(8,128)(2,1)}, f32[3,64,128]{2,1,0:T(8,128)}, bf1...) custom-call(s32[3]{0:T(128)} %phases.3, ...), custom_call_target="tpu_custom_call" | custom-call | tf_op jit(solution)/shard_map/front/pallas_call | solution.py:503
  46.0 6.3 %back.1 = (bf16[1,3,64,2048]{3,2,1,0:T(8,128)(2,1)}, bf16[1,3,64,2048]{3,2,1,0:T(8,128)(2,1)}, bf16[1,3,64,2048]{3,2,1,0:T(8,128)(2,1)}, f32[192,768]{1,0:T(8,128)}) custom-call(s32[3]{0:T(128)} %phases.3, s32[1]{0:T(128)S(6)} %copy.11.valid, bf16[3,64,2048]{2,1,0:T(8,128)(2,1)} %get-tuple-element.12.aq_hbm, bf16[3,64,2048]{2,1,0:T(8,128)(2,1)} %get-tuple-element.13.ak_hbm, ...), custom_call_target="tpu_custom_call" | custom-call | tf_op jit(solution)/shard_map/back/pallas_call | solution.py:530

commit v3 on v2

--- a/solution.py
+++ b/solution.py
@@ -271,9 +271,13 @@
     for h in range(HEADS):
         far_forward(h, 0)
 
-    do_out, do_in = gather(do_own, lambda n: do_far.at[core, n], qd_send, qd_recv, 7)
+    do_out, do_in = [], []
+    for h in range(HEADS):
+        sends, recvs = gather(do_own.at[h], lambda n, h=h: do_far.at[core, n, h], qd_send, qd_recv, 7 + 7 * h)
+        do_out += sends
+        do_in += recvs
     do_pair = to_pair(lambda c: do_far.at[c], HEADS + 1)
-    for c in do_out:
+    for c in do_out[:14]:
         c.start()
     do_copy = pltpu.make_async_copy(do_own, do_far.at[core, yx], own_sem.at[4])
     do_copy.start()
@@ -371,10 +375,10 @@
             half_s[...] = mine + a_recv[...].astype(F32)
             for t in range(4):
                 b_send[t] = half_s[(t // 2) * quarter:(t // 2 + 1) * quarter, (t % 2) * wide:(t % 2 + 1) * wide].astype(BF16)
-            for c in b_out:
+            for c in b_out + do_out[14:]:
                 c.start()
 
-        @pl.when(u == 3)
+        @pl.when(u == 1)
         def _():
             for c in b_in:
                 c.wait_recv()
@@ -386,12 +390,8 @@
             for c in c_out:
                 c.start()
 
-        @pl.when(u == 4)
+        @pl.when(u == 3)
         def _():
-            for c in do_in:
-                c.wait_recv()
-            do_copy.wait()
-            do_pair[0].start()
             for c in c_in:
                 c.wait_recv()
             total = c_buf[0].astype(F32)
@@ -401,6 +401,13 @@
             for c in d_out:
                 c.start()
             d_copy.start()
+
+        @pl.when(u == 4)
+        def _():
+            for c in do_in:
+                c.wait_recv()
+            do_copy.wait()
+            do_pair[0].start()
 
         return carry
 
@@ -459,31 +466,33 @@
         dscore = dprob.astype(BF16) * probs
         return jnp.concatenate([nt(dscore, q_t) * SCALE, nt(probs, do_t)], 1).T
 
-    for c in copies[:3]:
+    outs = []
+
+    def finish(n, near, far, out, dest):
+        for h in range(HEADS):
+            parts = place_parts(far[h], phases[h])
+            for c in range(16):
+                cols = pl.ds(c * 128, 128)
+                placed = jnp.where(place_mask(phases[h], c), parts[c // 4], 0.0)
+                out[h, :, cols] = (near[h, :, cols].astype(F32) + placed).astype(BF16)
+        outs.append(pltpu.make_async_copy(out, dest.at[0], out_sem.at[n]))
+        outs[-1].start()
+
+    for c in copies[:5]:
         c.wait()
+    finish(0, aq_s, fq_s, oq_s, dq_hbm)
     both = [far_backward_kv(h) for h in range(HEADS)]
-    for c in copies[3:]:
+    for c in copies[5:]:
         c.wait()
-    outs = []
-    for h in range(HEADS):
-        ph = phases[h]
-        parts_k, parts_v = place_parts(both[h][:DH], ph), place_parts(both[h][DH:], ph)
-        parts_q = place_parts(fq_s[h], ph)
-        for c in range(16):
-            cols = pl.ds(c * 128, 128)
-            mask = place_mask(ph, c)
-            for out, near, parts in ((oq_s, aq_s, parts_q), (ok_s, ak_s, parts_k), (ov_s, av_s, parts_v)):
-                out[h, :, cols] = (near[h, :, cols].astype(F32) + jnp.where(mask, parts[c // 4], 0.0)).astype(BF16)
-        for n, (a, b) in enumerate(((oq_s, dq_hbm), (ok_s, dk_hbm), (ov_s, dv_hbm))):
-            outs.append(pltpu.make_async_copy(a.at[h], b.at[0, h], out_sem.at[n, h]))
-            outs[-1].start()
+    finish(1, ak_s, [b[:DH] for b in both], ok_s, dk_hbm)
     half, quarter, wide = HEADS * DH // 2, HEADS * DH // 4, D // 2
     for cc in range(2):
         for t in range(4):
             gw_s[cc * half + (t // 2) * quarter:cc * half + (t // 2 + 1) * quarter, (t % 2) * wide:(t % 2 + 1) * wide] = (
                 d_buf[cc, t].astype(F32))
-    outs.append(pltpu.make_async_copy(gw_s, gw_hbm, out_sem.at[3, 0]))
+    outs.append(pltpu.make_async_copy(gw_s, gw_hbm, out_sem.at[3]))
     outs[-1].start()
+    finish(2, av_s, [b[DH:] for b in both], ov_s, dv_hbm)
     for c in outs:
         c.wait()
 
@@ -520,7 +529,7 @@
             pltpu.VMEM((HEADS * DH // 2, D), F32),
             pltpu.VMEM((4, *chunk), BF16), pltpu.VMEM((4, *chunk), BF16), pltpu.VMEM((4, *chunk), BF16),
             pltpu.VMEM(chunk, BF16),
-            dma((5,)), dma((3, HEADS)), dma((7,)), dma((21,)), dma((21,)), dma((14,)), dma((14,)), dma((5,)), dma((5,)),
+            dma((5,)), dma((3, HEADS)), dma((7,)), dma((21,)), dma((21,)), dma((28,)), dma((28,)), dma((5,)), dma((5,)),
             dma((2,)), dma((3,)), dma((3,)), dma((3,)), dma((3,)), dma((7,)), dma((7,)),
         ],
         compiler_params=pltpu.CompilerParams(
@@ -533,7 +542,7 @@
         in_specs=[smem, smem] + [any_spec] * 8,
         out_specs=[any_spec] * 4,
         scratch_shapes=[pltpu.VMEM(p.shape, p.dtype) for p in passed] + [
-            big(BF16), big(BF16), big(BF16), pltpu.VMEM((HEADS * DH, D), F32), dma((8,)), dma((4, HEADS))],
+            big(BF16), big(BF16), big(BF16), pltpu.VMEM((HEADS * DH, D), F32), dma((8,)), dma((4,))],
         compiler_params=pltpu.CompilerParams(vmem_limit_bytes=58 << 20),
         name="back",
     )(phases, valid_rows, *between)

time: 52.6 us -> 50.8 us (0.966)
  Pallas kernels: 51 us -> 49.2 us
    pallas_call x1, Pallas kernels: 44.7 us -> 42.8 us  [shards(): pl.pallas_call(front_kernel, out_shape=passed, in_specs=[smem, smem] + [a...]
where the time goes in v3:
time: 50.8 us; the launch traced here: 50.6 us
  Pallas kernels  49.2 us (97%)
  between operations  1.45 us (3%)
    pallas_call x1, Pallas kernels, shards(): pl.pallas_call(front_kernel, out_shape=passed, in_specs=[smem, smem] + [a...  42.8 us
    pallas_call x1, Pallas kernels, shards(): pl.pallas_call(back_kernel, out_shape=[state, state, state, shape((HEADS...  6.41 us

profile of v3, /device:TPU:1, one launch (start us, length us, event | category | flops | bytes accessed | tf_op | source)
XLA Modules:
  0.0 50.6 jit_solution(16770102297786662507)
XLA Ops:
  1.3 42.8 %front.1 = (bf16[3,64,2048]{2,1,0:T(8,128)(2,1)}, bf16[3,64,2048]{2,1,0:T(8,128)(2,1)}, bf16[3,64,2048]{2,1,0:T(8,128)(2,1)}, f32[3,64,128]{2,1,0:T(8,128)}, bf1...) custom-call(s32[3]{0:T(128)} %phases.3, ...), custom_call_target="tpu_custom_call" | custom-call | tf_op jit(solution)/shard_map/front/pallas_call | solution.py:512
  44.1 6.4 %back.1 = (bf16[1,3,64,2048]{3,2,1,0:T(8,128)(2,1)}, bf16[1,3,64,2048]{3,2,1,0:T(8,128)(2,1)}, bf16[1,3,64,2048]{3,2,1,0:T(8,128)(2,1)}, f32[192,768]{1,0:T(8,128)}) custom-call(s32[3]{0:T(128)} %phases.3, s32[1]{0:T(128)S(6)} %copy.11.valid, bf16[3,64,2048]{2,1,0:T(8,128)(2,1)} %get-tuple-element.12.aq_hbm, bf16[3,64,2048]{2,1,0:T(8,128)(2,1)} %get-tuple-element.13.ak_hbm, ...), custom_call_target="tpu_custom_call" | custom-call | tf_op jit(solution)/shard_map/back/pallas_call | solution.py:539

commit v4 on v3

--- a/solution.py
+++ b/solution.py
@@ -87,7 +87,7 @@
     phases, valid, q_hbm, k_hbm, v_hbm, w_hbm, go_hbm,
     aq_hbm, ak_hbm, av_hbm, fq_hbm, own_hbm, q_far, do_far, d_far,
     q_s, k_s, v_s, w_s, go_s, g_s, e_s, ds_s, on_s, st_s, nd_s, at_s,
-    kv_buf, q_own, do_own, fe_s, fq_s, fr_s, aq_s, ak_s, av_s,
+    kv_buf, q_own, do_own, gp_s, fe_s, fq_s, fr_s, aq_s, ak_s, av_s,
     gw_s, a_send, a_recv, half_s, b_send, b_recv, c_buf, d_own,
     in_sem, out_sem, own_sem, kv_send, kv_recv, qd_send, qd_recv, pair_send, pair_recv,
     a_sem, b_ss, b_rs, c_ss, c_rs, d_ss, d_rs,
@@ -132,8 +132,8 @@
         c.wait()
     for h in range(HEADS):
         ph = phases[h]
-        kv_buf[core, h, yx, 0:DH, :] = pick(lambda o: k_s[h, :, pl.ds(o, 128)], ph).astype(BF16)
-        kv_buf[core, h, yx, DH:2 * DH, :] = pick(lambda o: v_s[h, :, pl.ds(o, 128)], ph).astype(BF16)
+        kv_buf[core, 0, yx, h] = pick(lambda o: k_s[h, :, pl.ds(o, 128)], ph).astype(BF16)
+        kv_buf[core, 1, yx, h] = pick(lambda o: v_s[h, :, pl.ds(o, 128)], ph).astype(BF16)
     pl.semaphore_wait(barrier, len(greet))
 
     def gather(mine, slot, ss, rs, base):
@@ -154,11 +154,11 @@
         return out, back
 
     kv_out, kv_in, kv_pair = [], [], []
-    for h in range(HEADS):
-        sends, recvs = gather(kv_buf.at[core, h, yx], lambda n, h=h: kv_buf.at[core, h, n], kv_send, kv_recv, 7 * h)
+    for t in range(2):
+        sends, recvs = gather(kv_buf.at[core, t, yx], lambda n, t=t: kv_buf.at[core, t, n], kv_send, kv_recv, 7 * t)
         kv_out.append(sends)
         kv_in.append(recvs)
-        kv_pair.append(to_pair(lambda c, h=h: kv_buf.at[c, h], h))
+        kv_pair.append(to_pair(lambda c, t=t: kv_buf.at[c, t], t))
         for c in sends:
             c.start()
 
@@ -166,7 +166,7 @@
     for h in range(HEADS):
         q_own[h] = pick(lambda o: q_s[h, :, pl.ds(o, 128)], phases[h]).astype(BF16)
     own_copies = [
-        pltpu.make_async_copy(kv_buf.at[core, h, yx], own_hbm.at[h], own_sem.at[h]) for h in range(HEADS)]
+        pltpu.make_async_copy(kv_buf.at[core, t, yx], own_hbm.at[t], own_sem.at[t]) for t in range(2)]
     own_copies.append(pltpu.make_async_copy(q_own, q_far.at[core, yx], own_sem.at[3]))
     for c in own_copies:
         c.start()
@@ -196,26 +196,40 @@
 
     for u in range(2 * HEADS):
         near_forward(u, 0)
-        if u == 3:
-            forward_pair(0)
-    forward_pair(1)
+    forward_pair(0)
     copies[3].wait()
     copies[4].wait()
     g_s[...] = nt(w_s[...], go_s[...]).astype(BF16).reshape(HEADS, DH, ROWS)
-    forward_pair(2)
+    for h in range(HEADS):
+        for c in range(16):
+            cols = pl.ds(c * 128, 128)
+            near = on_s[h, :, cols]
+            rr = st_s[h, 0:1, cols]
+            nd = (g_s[h, :, cols].astype(F32) * rr).astype(BF16)
+            nd_s[h, :, cols] = nd
+            st_s[h, 2:3, cols] = -jnp.sum(nd.astype(F32) * near, axis=0, keepdims=True)
+            at_s[h, :, cols] = jnp.where(place_mask(phases[h], c), 0.0, near).astype(BF16)
+    forward_pair(1)
+    gw_s[...] = nn(at_s[...].reshape(HEADS * DH, ROWS), go_s[...])
     q_out, q_in = gather(q_own, lambda n: q_far.at[core, n], qd_send, qd_recv, 0)
     q_pair = to_pair(lambda c: q_far.at[c], HEADS)
     for c in q_out:
         c.start()
 
+    for h in range(HEADS):
+        which = jnp.full((1, D), phases[h], jnp.int32)
+        for b in range(4):
+            rows = [go_s[b * 512 + n * BLK:b * 512 + (n + 1) * BLK, :] for n in range(RATE)]
+            gp_s[h, b * BLK:(b + 1) * BLK, :] = choose(rows, which)
+
     key_index = lanes(SPAN)
 
-    def all_cols(buf, h, lo, hi):
-        return jnp.concatenate([buf[n % 2, h, n // 2, lo:hi, :] for n in range(PEERS)], 1)
-
-    def far_forward(h, carry):
+    def all_cols(t, h):
+        return jnp.concatenate([kv_buf[n % 2, t, n // 2, h] for n in range(PEERS)], 1)
+
+    def far_scores(h):
         ph = phases[h]
-        k_t, v_t = all_cols(kv_buf, h, 0, DH), all_cols(kv_buf, h, DH, 2 * DH)
+        k_t = all_cols(0, h)
         q_t = q_own[h].astype(F32) * (SCALE * LOG2E)
         hi = q_t.astype(BF16).astype(F32)
         lhs = jnp.concatenate([hi, q_t - hi], 0).T.astype(BF16)
@@ -225,6 +239,11 @@
         m = jnp.max(s, axis=1, keepdims=True)
         e = jnp.exp2(s - m).astype(BF16)
         fe_s[h] = e
+        return m
+
+    def far_forward(h, m):
+        ph = phases[h]
+        e, v_t = fe_s[h], all_cols(1, h)
         o = nt(e, jnp.concatenate([v_t, jnp.ones((16, SPAN), BF16)], 0))
         total = o[:, DH:DH + 1]
         r = 1.0 / total
@@ -232,7 +251,8 @@
             [o[:, :DH] * r, jnp.broadcast_to(m + jnp.log2(total), (SUB, 32)), jnp.broadcast_to(r, (SUB, 32))], 1).T
         far_out, far_lse, far_r = packed[0:DH], packed[DH:DH + 1], packed[96:97]
         near_out = pick(lambda o: on_s[h, :, pl.ds(o, 128)], ph)
-        near_lse = pick(lambda o: st_s[h, :, pl.ds(o, 128)], ph)[1:2]
+        near_stats = pick(lambda o: st_s[h, :, pl.ds(o, 128)], ph)
+        near_r, near_lse = near_stats[0:1], near_stats[1:2]
         g = pick(lambda o: g_s[h, :, pl.ds(o, 128)], ph)
         mixing = 1.0 / (1.0 + jnp.exp2(near_lse - far_lse))
         rest = 1.0 / (1.0 + jnp.exp2(far_lse - near_lse))
@@ -249,27 +269,23 @@
         term_r = far_dlse * far_r - jnp.sum(scaled * far_out, axis=0, keepdims=True)
         fr_s[h, 0:DH, :] = scaled
         fr_s[h, DH:DH + 8, :] = jnp.broadcast_to(term_r, (8, SUB))
-        stack = jnp.concatenate([comb, rest, -far_dlse, jnp.zeros((6, SUB), F32)], 0)
-        parts = place_parts(stack, ph)
+        gw_s[h * DH:(h + 1) * DH, :] += nn(comb.astype(BF16), gp_s[h])
+        near_dout = (rest * g).astype(BF16).astype(F32)
+        nd = (near_dout * near_r).astype(BF16).astype(F32)
+        near_term = -far_dlse * near_r - jnp.sum(nd * near_out, axis=0, keepdims=True)
+        parts = place_parts(jnp.concatenate([nd, near_term, jnp.zeros((7, SUB), F32)], 0), ph)
         for c in range(16):
             cols = pl.ds(c * 128, 128)
             mask = place_mask(ph, c)
             part = parts[c // 4]
-            near = on_s[h, :, cols]
-            at_s[h, :, cols] = jnp.where(mask, part[:DH], near).astype(BF16)
-            factor = jnp.where(mask, part[DH:DH + 1], 1.0)
-            dlse = jnp.where(mask, part[DH + 1:DH + 2], 0.0)
-            rr = st_s[h, 0:1, cols]
-            nd = (g_s[h, :, cols].astype(F32) * factor).astype(BF16).astype(F32)
-            nd = (nd * rr).astype(BF16)
-            nd_s[h, :, cols] = nd
-            st_s[h, 2:3, cols] = dlse * rr - jnp.sum(nd.astype(F32) * near, axis=0, keepdims=True)
-        return carry
-
-    for h in range(HEADS):
-        kv_pair[h][1].wait_recv()
-    for h in range(HEADS):
-        far_forward(h, 0)
+            nd_s[h, :, cols] = jnp.where(mask, part[:DH], nd_s[h, :, cols].astype(F32)).astype(BF16)
+            st_s[h, 2:3, cols] = jnp.where(mask, part[DH:DH + 1], st_s[h, 2:3, cols])
+
+    kv_pair[0][1].wait_recv()
+    tops = [far_scores(h) for h in range(HEADS)]
+    kv_pair[1][1].wait_recv()
+    for h in range(HEADS):
+        far_forward(h, tops[h])
 
     do_out, do_in = [], []
     for h in range(HEADS):
@@ -282,14 +298,13 @@
     do_copy = pltpu.make_async_copy(do_own, do_far.at[core, yx], own_sem.at[4])
     do_copy.start()
 
-    gw_s[...] = nn(at_s[...].reshape(HEADS * DH, ROWS), go_s[...])
     half = HEADS * DH // 2
     a_send[...] = gw_s[pl.ds(pl.multiple_of((1 - core) * half, 32), half), :].astype(BF16)
     a_copy = pltpu.make_async_remote_copy(a_send, a_recv, a_sem.at[0], a_sem.at[1], device_id=sibling, device_id_type=MESH)
     a_copy.start()
 
     def far_backward_q(h, carry):
-        k_t, v_t = all_cols(kv_buf, h, 0, DH), all_cols(kv_buf, h, DH, 2 * DH)
+        k_t, v_t = all_cols(0, h), all_cols(1, h)
         d = fr_s[h]
         term = d[DH:DH + 1]
         term_hi = term.astype(BF16).astype(F32)
@@ -449,8 +464,8 @@
         ph = phases[h]
         q_t, do_t = all_cols(q_buf, h, 0, DH), all_cols(do_buf, h, 0, DH)
         stats = all_cols(do_buf, h, DH, DO_ROWS)
-        own_k = own_s[h, 0:DH, :].astype(F32) * (SCALE * LOG2E)
-        own_v = own_s[h, DH:2 * DH, :].astype(F32)
+        own_k = own_s[0, h].astype(F32) * (SCALE * LOG2E)
+        own_v = own_s[1, h].astype(F32)
         hi = own_k.astype(BF16).astype(F32)
         index = lax.broadcasted_iota(jnp.int32, (16, SUB), 0)
         first = jnp.where(index < 3, 1.0, 0.0)
@@ -507,7 +522,7 @@
     near = jax.ShapeDtypeStruct((HEADS, DH, ROWS), BF16)
     shape = jax.ShapeDtypeStruct
     passed = [
-        near, near, near, shape((HEADS, DH, SUB), F32), shape((HEADS, 2 * DH, SUB), BF16),
+        near, near, near, shape((HEADS, DH, SUB), F32), shape((2, HEADS, DH, SUB), BF16),
         shape((2, 8, HEADS, DH, SUB), BF16), shape((2, 8, HEADS, DO_ROWS, SUB), BF16), shape((2, 4, *chunk), BF16)]
     between = pl.pallas_call(
         front_kernel,
@@ -520,8 +535,9 @@
             big(BF16),
             pltpu.VMEM((2 * HEADS, SEG, SEG), BF16), pltpu.VMEM((SEG, SEG), BF16),
             big(F32), pltpu.VMEM((HEADS, 8, ROWS), F32), big(BF16), big(BF16),
-            pltpu.VMEM((2, HEADS, 8, 2 * DH, SUB), BF16),
+            pltpu.VMEM((2, 2, 8, HEADS, DH, SUB), BF16),
             pltpu.VMEM((HEADS, DH, SUB), BF16), pltpu.VMEM((HEADS, DO_ROWS, SUB), BF16),
+            pltpu.VMEM((HEADS, SUB, D), BF16),
             pltpu.VMEM((HEADS, SUB, SPAN), BF16), pltpu.VMEM((HEADS, DH, SUB), F32), pltpu.VMEM((HEADS, DH + 8, SUB), F32),
             big(BF16), big(BF16), big(BF16),
             pltpu.VMEM((HEADS * DH, D), F32),

time: 50.8 us -> 49.5 us (0.974)
  Pallas kernels: 49.2 us -> 47.9 us
    pallas_call x1, Pallas kernels: 42.8 us -> 41.5 us  [shards(): pl.pallas_call(front_kernel, out_shape=passed, in_specs=[smem, smem] + [a...]
where the time goes in v4:
time: 49.5 us; the launch traced here: 49.3 us
  Pallas kernels  47.9 us (97%)
  between operations  1.45 us (3%)
    pallas_call x1, Pallas kernels, shards(): pl.pallas_call(front_kernel, out_shape=passed, in_specs=[smem, smem] + [a...  41.5 us
    pallas_call x1, Pallas kernels, shards(): pl.pallas_call(back_kernel, out_shape=[state, state, state, shape((HEADS...  6.43 us

profile of v4, /device:TPU:1, one launch (start us, length us, event | category | flops | bytes accessed | tf_op | source)
XLA Modules:
  0.0 49.3 jit_solution(7901771988025299661)
XLA Ops:
  1.3 41.5 %front.1 = (bf16[3,64,2048]{2,1,0:T(8,128)(2,1)}, bf16[3,64,2048]{2,1,0:T(8,128)(2,1)}, bf16[3,64,2048]{2,1,0:T(8,128)(2,1)}, f32[3,64,128]{2,1,0:T(8,128)}, bf1...) custom-call(s32[3]{0:T(128)} %phases.3, ...), custom_call_target="tpu_custom_call" | custom-call | tf_op jit(solution)/shard_map/front/pallas_call | solution.py:527
  42.7 6.4 %back.1 = (bf16[1,3,64,2048]{3,2,1,0:T(8,128)(2,1)}, bf16[1,3,64,2048]{3,2,1,0:T(8,128)(2,1)}, bf16[1,3,64,2048]{3,2,1,0:T(8,128)(2,1)}, f32[192,768]{1,0:T(8,128)}) custom-call(s32[3]{0:T(128)} %phases.3, s32[1]{0:T(128)S(6)} %copy.11.valid, bf16[3,64,2048]{2,1,0:T(8,128)(2,1)} %get-tuple-element.12.aq_hbm, bf16[3,64,2048]{2,1,0:T(8,128)(2,1)} %get-tuple-element.13.ak_hbm, ...), custom_call_target="tpu_custom_call" | custom-call | tf_op jit(solution)/shard_map/back/pallas_call | solution.py:555

commit v5 on v4

--- a/solution.py
+++ b/solution.py
@@ -128,17 +128,17 @@
     for peer in greet:
         pl.semaphore_signal(barrier, inc=1, device_id=peer, device_id_type=MESH)
 
-    for c in copies[:2]:
-        c.wait()
-    for h in range(HEADS):
-        ph = phases[h]
-        kv_buf[core, 0, yx, h] = pick(lambda o: k_s[h, :, pl.ds(o, 128)], ph).astype(BF16)
-        kv_buf[core, 1, yx, h] = pick(lambda o: v_s[h, :, pl.ds(o, 128)], ph).astype(BF16)
+    def pick_into(t, ref):
+        copies[t].wait()
+        for h in range(HEADS):
+            kv_buf[core, t, yx, h] = pick(lambda o: ref[h, :, pl.ds(o, 128)], phases[h]).astype(BF16)
+
+    pick_into(0, k_s)
     pl.semaphore_wait(barrier, len(greet))
 
     def gather(mine, slot, ss, rs, base):
         sends, recvs = [], []
-        for k in range(1, 8):
+        for k in (6, 2, 5, 7, 1, 3, 4):
             n = base + k - 1
             sends.append(pltpu.make_async_remote_copy(
                 mine, slot(yx), ss.at[n], rs.at[n], device_id=same_core[k - 1], device_id_type=MESH))
@@ -155,6 +155,8 @@
 
     kv_out, kv_in, kv_pair = [], [], []
     for t in range(2):
+        if t == 1:
+            pick_into(1, v_s)
         sends, recvs = gather(kv_buf.at[core, t, yx], lambda n, t=t: kv_buf.at[core, t, n], kv_send, kv_recv, 7 * t)
         kv_out.append(sends)
         kv_in.append(recvs)

time: 49.5 us -> 48.9 us (0.988)
  Pallas kernels: 47.9 us -> 47.3 us
    pallas_call x1, Pallas kernels: 41.5 us -> 40.9 us  [shards(): pl.pallas_call(front_kernel, out_shape=passed, in_specs=[smem, smem] + [a...]
where the time goes in v5:
time: 48.9 us; the launch traced here: 48.7 us
  Pallas kernels  47.3 us (97%)
  between operations  1.45 us (3%)
    pallas_call x1, Pallas kernels, shards(): pl.pallas_call(front_kernel, out_shape=passed, in_specs=[smem, smem] + [a...  40.9 us
    pallas_call x1, Pallas kernels, shards(): pl.pallas_call(back_kernel, out_shape=[state, state, state, shape((HEADS...  6.41 us

profile of v5, /device:TPU:1, one launch (start us, length us, event | category | flops | bytes accessed | tf_op | source)
XLA Modules:
  0.0 48.7 jit_solution(15321205303289144575)
XLA Ops:
  1.3 40.9 %front.1 = (bf16[3,64,2048]{2,1,0:T(8,128)(2,1)}, bf16[3,64,2048]{2,1,0:T(8,128)(2,1)}, bf16[3,64,2048]{2,1,0:T(8,128)(2,1)}, f32[3,64,128]{2,1,0:T(8,128)}, bf1...) custom-call(s32[3]{0:T(128)} %phases.3, ...), custom_call_target="tpu_custom_call" | custom-call | tf_op jit(solution)/shard_map/front/pallas_call | solution.py:529
  42.2 6.4 %back.1 = (bf16[1,3,64,2048]{3,2,1,0:T(8,128)(2,1)}, bf16[1,3,64,2048]{3,2,1,0:T(8,128)(2,1)}, bf16[1,3,64,2048]{3,2,1,0:T(8,128)(2,1)}, f32[192,768]{1,0:T(8,128)}) custom-call(s32[3]{0:T(128)} %phases.3, s32[1]{0:T(128)S(6)} %copy.11.valid, bf16[3,64,2048]{2,1,0:T(8,128)(2,1)} %get-tuple-element.12.aq_hbm, bf16[3,64,2048]{2,1,0:T(8,128)(2,1)} %get-tuple-element.13.ak_hbm, ...), custom_call_target="tpu_custom_call" | custom-call | tf_op jit(solution)/shard_map/back/pallas_call | solution.py:557

commit v6 on v5

--- a/solution.py
+++ b/solution.py
@@ -138,7 +138,7 @@
 
     def gather(mine, slot, ss, rs, base):
         sends, recvs = [], []
-        for k in (6, 2, 5, 7, 1, 3, 4):
+        for k in (6, 5, 7, 2, 4, 1, 3):
             n = base + k - 1
             sends.append(pltpu.make_async_remote_copy(
                 mine, slot(yx), ss.at[n], rs.at[n], device_id=same_core[k - 1], device_id_type=MESH))

time: 48.9 us -> 49.1 us (level)
  no operation moved by 1% of the time
where the time goes in v6:
time: 49.1 us; the launch traced here: 48.9 us
  Pallas kernels  47.5 us (97%)
  between operations  1.45 us (3%)
    pallas_call x1, Pallas kernels, shards(): pl.pallas_call(front_kernel, out_shape=passed, in_specs=[smem, smem] + [a...  41.1 us
    pallas_call x1, Pallas kernels, shards(): pl.pallas_call(back_kernel, out_shape=[state, state, state, shape((HEADS...  6.42 us

profile of v6, /device:TPU:1, one launch (start us, length us, event | category | flops | bytes accessed | tf_op | source)
XLA Modules:
  0.0 48.9 jit_solution(10316322612777854198)
XLA Ops:
  1.3 41.1 %front.1 = (bf16[3,64,2048]{2,1,0:T(8,128)(2,1)}, bf16[3,64,2048]{2,1,0:T(8,128)(2,1)}, bf16[3,64,2048]{2,1,0:T(8,128)(2,1)}, f32[3,64,128]{2,1,0:T(8,128)}, bf1...) custom-call(s32[3]{0:T(128)} %phases.3, ...), custom_call_target="tpu_custom_call" | custom-call | tf_op jit(solution)/shard_map/front/pallas_call | solution.py:529
  42.4 6.4 %back.1 = (bf16[1,3,64,2048]{3,2,1,0:T(8,128)(2,1)}, bf16[1,3,64,2048]{3,2,1,0:T(8,128)(2,1)}, bf16[1,3,64,2048]{3,2,1,0:T(8,128)(2,1)}, f32[192,768]{1,0:T(8,128)}) custom-call(s32[3]{0:T(128)} %phases.3, s32[1]{0:T(128)S(6)} %copy.11.valid, bf16[3,64,2048]{2,1,0:T(8,128)(2,1)} %get-tuple-element.12.aq_hbm, bf16[3,64,2048]{2,1,0:T(8,128)(2,1)} %get-tuple-element.13.ak_hbm, ...), custom_call_target="tpu_custom_call" | custom-call | tf_op jit(solution)/shard_map/back/pallas_call | solution.py:557
